TPU v7x, 32 devices: a whole 2x2x4 slice. The times are simulated.
32 devices in a mesh: fsdp: 4 (over y, x), context: 4 (over z), tensor: 2 (over core).
Axes of the slice: x: 2, y: 2, z: 4, core: 2. Of those that a mesh axis runs over, the one named last changes fastest.
Arguments:
- tokens: bfloat16 [4, 2560, 768], P('fsdp', 'context'), may hold values from -6 to 6
- attn_gain: bfloat16 [768], P('fsdp'), may hold values from 0.5 to 1.5
- w_qkv: bfloat16 [768, 3, 768], P('fsdp', None, 'tensor'), may hold values from -0.21875 to 0.21875
- w_out: bfloat16 [768, 768], P('tensor', 'fsdp'), may hold values from -0.875 to 0.875
- ffn_gain: bfloat16 [768], P('fsdp'), may hold values from 0.5 to 1.5
- w_gu: bfloat16 [768, 2, 2048], P('fsdp', None, 'tensor'), may hold values from -0.21875 to 0.21875
- w_dn: bfloat16 [2048, 768], P('tensor', 'fsdp'), may hold values from -0.125 to 0.125
- w_egu: bfloat16 [8, 768, 2, 2048], P('fsdp', None, None, 'tensor'), may hold values from -0.21875 to 0.21875
- w_edn: bfloat16 [8, 2048, 768], P('fsdp', 'tensor'), may hold values from -0.125 to 0.125
- adapters: bfloat16 [8, 233472], P('fsdp', ('context', 'tensor')), may hold values from -0.29882812 to 0.29882812
- adapter_ids: int32 [4], P('fsdp'), may hold values from 0 to 7
- parents: int32 [4, 13], P('fsdp'), may hold values from 0 to 4, as said below
- seg_lengths: int32 [4, 13], P('fsdp'), may hold values from 64 to 1024, as said below
- routes: int32 [4, 2560, 2], P('fsdp', 'context'), may hold values from 0 to 7, as said below
- route_weights: bfloat16 [4, 2560, 2], P('fsdp', 'context'), may hold values from 0.25 to 0.75
- cotangent: bfloat16 [4, 2560, 768], P('fsdp', 'context'), may hold values from -6 to 6
Outputs:
- block_out: float32 [4, 2560, 768], P('fsdp', 'context')
- input_grad: float32 [4, 2560, 768], P('fsdp', 'context')
- adapter_grads: float32 [8, 233472], P('fsdp', ('context', 'tensor'))
Inputs may be any that keep to these rules, and one draw needn't show every extreme that they name: Segment 0 is the root with parent 0; segments 1 to 4 have parent 0; segments 5 to 12 have parents among 1 to 4, two each. `seg_lengths`: segment 0 has 1024 tokens; every other segment has 64 to 192; a tree's lengths sum to 2560. `routes`: a token's two experts differ; among the rows that one device holds (640 rows of each of its 1 trees) no expert is named more than 320 times, and one expert is named exactly 320 times.
All inputs are finite; a program needn't handle non-finite values.
Results may differ from a plain program's by a relative error of at most 0.02.
The roundings to bfloat16 on the way count: a program that leaves them out, or rounds other values in their place, can miss the bound.
Values may be sent and summed in bfloat16 or wider, within the bound.
A program may use at most 320 MiB of HBM per device.

v0:
```python
import jax
import jax.numpy as jnp
import functools
import math

from jax import lax
from jax.experimental import pallas as pl
from jax.experimental.pallas import tpu as pltpu
from jax.sharding import PartitionSpec as P

D = 768
HEADS = 12
HEAD_DIM = 64
FF = 2048
EXPERTS = 8
TOPK = 2
RANK = 16
ADAPTERS = 8
PARAMS = 233472


epsilon = 1e-06
adapter_scale = 2.0
rope_base = 10000.0
masked_score = -1e30
highest_precision = lax.Precision.HIGHEST


def rms_scale(values):
    return lax.rsqrt(jnp.mean(values * values, axis=-1, keepdims=True) + epsilon)


def norm_back(values, scaling, gain_values, gradient):
    weighted = gradient * gain_values
    inner_mean = jnp.mean(values * weighted, axis=-1, keepdims=True)
    return scaling * weighted - values * (scaling * scaling * scaling) * inner_mean


SLOT_TILE = 512
TOKEN_TILE = 256
SLOT_WINDOW = 128


def nt_dot(left, right):
    return lax.dot_general(left, right, (((1,), (1,)), ((), ())), preferred_element_type=jnp.float32)


def tn_dot(left, right):
    return lax.dot_general(left, right, (((0,), (0,)), ((), ())), preferred_element_type=jnp.float32)


def nn_dot(left, right):
    return jnp.dot(left, right, preferred_element_type=jnp.float32)


def moe_kernel(
    starts,
    place_row,
    place_hbm,
    weight_hbm,
    rows_hbm,
    grads_hbm,
    egu_hbm,
    edn_hbm,
    out_hbm,
    back_hbm,
    place_col,
    weight_col,
    rows_ref,
    grads_ref,
    egu_ref,
    edn_ref,
    out_ref,
    back_ref,
    taken,
    taken_grad,
    taken_weight,
    sems,
    block_sems,
):
    f32, bf = jnp.float32, jnp.bfloat16
    experts = egu_hbm.shape[0]
    blocks = rows_ref.shape[0] // TOKEN_TILE

    def block_rows(b):
        return pl.ds(pl.multiple_of(b * TOKEN_TILE, TOKEN_TILE), TOKEN_TILE)

    def loads(b):
        block = block_rows(b)
        return [
            pltpu.make_async_copy(source.at[block], target.at[block], block_sems.at[i, b])
            for i, (source, target) in enumerate(
                ((rows_hbm, rows_ref), (grads_hbm, grads_ref), (weight_hbm, weight_col))
            )
        ]

    def stores(b):
        block = block_rows(b)
        return [
            pltpu.make_async_copy(source.at[block], target.at[block], block_sems.at[3 + i, b])
            for i, (source, target) in enumerate(((out_ref, out_hbm), (back_ref, back_hbm)))
        ]

    def weights(e):
        return [
            pltpu.make_async_copy(egu_hbm.at[e], egu_ref.at[e], sems.at[0, e]),
            pltpu.make_async_copy(edn_hbm.at[e], edn_ref.at[e], sems.at[1, e]),
        ]

    def each(count, copies, action):
        def step(i, carry):
            for copy in copies(i):
                getattr(copy, action)()
            return carry

        lax.fori_loop(0, count, step, 0)

    each(blocks, loads, "start")
    each(experts, weights, "start")
    place_copy = pltpu.make_async_copy(place_hbm, place_col, sems.at[2, 0])
    place_copy.start()
    taken[...] = jnp.zeros_like(taken)
    taken_grad[...] = jnp.zeros_like(taken_grad)
    taken_weight[...] = jnp.zeros_like(taken_weight)
    slot_rows = lax.broadcasted_iota(jnp.int32, (SLOT_WINDOW, TOKEN_TILE), 0).astype(f32)
    slot_cols = lax.broadcasted_iota(jnp.int32, (TOKEN_TILE, SLOT_WINDOW), 1).astype(f32)

    def windows(e, b):
        begin = starts[e, b] // 16 * 16
        return begin, (starts[e, b + 1] - begin + SLOT_WINDOW - 1) // SLOT_WINDOW

    def window_rows(begin, i):
        return pl.ds(pl.multiple_of(begin + i * SLOT_WINDOW, 16), SLOT_WINDOW)

    def fetch(b, carry):
        block = block_rows(b)
        for copy in loads(b):
            copy.wait()

        def take(which):
            picks = []
            for e, first in which:
                hit = place_row[e : e + 1, block] == slot_rows + first.astype(f32)
                picks.append(jnp.where(hit, 1.0, 0.0).astype(bf))
            pick = picks[0] if len(picks) == 1 else jnp.concatenate(picks, axis=0)
            for source, target in (
                (rows_ref, taken),
                (grads_ref, taken_grad),
                (weight_col, taken_weight),
            ):
                got = nn_dot(pick, source[block, :]).astype(bf)
                for i, (e, first) in enumerate(which):
                    slots = window_rows(first, 0)
                    target[e, slots, :] += got[i * SLOT_WINDOW : (i + 1) * SLOT_WINDOW, :]

        spans = [windows(e, b) for e in range(experts)]
        take([(e, spans[e][0]) for e in range(experts)])
        for e in range(experts):

            def more(i, c, e=e):
                take([(e, spans[e][0] + i * SLOT_WINDOW)])
                return c

            lax.fori_loop(1, spans[e][1], more, 0)
        return carry

    lax.fori_loop(0, blocks, fetch, 0)

    def tile(e, start, size):
        slots = pl.ds(pl.multiple_of(start, 128), size)
        inputs = taken[e, slots, :]
        gate_pre = nn_dot(inputs, egu_ref[e, 0])
        up_pre = nn_dot(inputs, egu_ref[e, 1])
        sigmoid_gate = jax.nn.sigmoid(gate_pre)
        silu = gate_pre * sigmoid_gate
        active = (silu * up_pre).astype(bf)
        taken[e, slots, :] = nn_dot(active, edn_ref[e]).astype(bf)
        grad_active = nt_dot(taken_grad[e, slots, :], edn_ref[e])
        lane = lax.broadcasted_iota(jnp.int32, (size, 128), 1)
        scale = jnp.sum(
            jnp.where(lane == e, taken_weight[e, slots, :].astype(f32), 0.0), axis=1, keepdims=True
        )
        grad_active = grad_active * scale
        grad_gate = (
            grad_active * up_pre * sigmoid_gate * (1.0 + gate_pre * (1.0 - sigmoid_gate))
        ).astype(bf)
        grad_up = (grad_active * silu).astype(bf)
        taken_grad[e, slots, :] = (
            nt_dot(grad_gate, egu_ref[e, 0]) + nt_dot(grad_up, egu_ref[e, 1])
        ).astype(bf)

    def expert_step(e, carry):
        for copy in weights(e):
            copy.wait()
        count = starts[e, blocks]
        whole = count // SLOT_TILE
        rest = count - whole * SLOT_TILE

        def step(i, c):
            tile(e, i * SLOT_TILE, SLOT_TILE)
            return c

        lax.fori_loop(0, whole + jnp.where(rest > SLOT_TILE - 128, 1, 0), step, 0)
        for size in range(128, SLOT_TILE, 128):

            @pl.when((rest > size - 128) & (rest <= size))
            def _(size=size):
                tile(e, whole * SLOT_TILE, size)

        return carry

    lax.fori_loop(0, experts, expert_step, 0)
    place_copy.wait()

    def give(b, carry):
        block = block_rows(b)

        def hand(which):
            plain, scaled, values, values_grad = [], [], [], []
            for e, first in which:
                hit = place_col[block, e : e + 1] == slot_cols + first.astype(f32)
                plain.append(jnp.where(hit, 1.0, 0.0).astype(bf))
                weight = weight_col[block, e : e + 1].astype(f32)
                scaled.append(jnp.where(hit, weight, 0.0).astype(bf))
                values.append(taken[e, window_rows(first, 0), :])
                values_grad.append(taken_grad[e, window_rows(first, 0), :])

            def join(pieces, axis):
                return pieces[0] if len(pieces) == 1 else jnp.concatenate(pieces, axis=axis)

            return (
                nn_dot(join(scaled, 1), join(values, 0)),
                nn_dot(join(plain, 1), join(values_grad, 0)),
            )

        spans = [windows(e, b) for e in range(experts)]
        first, second = hand([(e, spans[e][0]) for e in range(experts)])
        out_ref[block, :] = first.astype(bf)
        back_ref[block, :] = second.astype(bf)
        for e in range(experts):

            def more(i, c, e=e):
                first, second = hand([(e, spans[e][0] + i * SLOT_WINDOW)])
                out_ref[block, :] = (out_ref[block, :].astype(f32) + first).astype(bf)
                back_ref[block, :] = (back_ref[block, :].astype(f32) + second).astype(bf)
                return c

            lax.fori_loop(1, spans[e][1], more, 0)
        for copy in stores(b):
            copy.start()
        return carry

    lax.fori_loop(0, blocks, give, 0)
    each(blocks, stores, "wait")


def moe_call(starts, place_row, place_col, weight_col, rows, grads, egu, edn):
    total, width = rows.shape
    experts = egu.shape[0]
    slots = total // 2 + SLOT_TILE
    blocks = total // TOKEN_TILE
    bf, f32 = jnp.bfloat16, jnp.float32
    vmem = pl.BlockSpec(memory_space=pltpu.VMEM)
    hbm = pl.BlockSpec(memory_space=pl.ANY)
    shape = jax.ShapeDtypeStruct((total, width), bf)
    return pl.pallas_call(
        moe_kernel,
        grid_spec=pltpu.PrefetchScalarGridSpec(
            num_scalar_prefetch=1,
            grid=(),
            in_specs=[vmem] + [hbm] * 6,
            out_specs=[hbm, hbm],
            scratch_shapes=[
                pltpu.VMEM((total, 128), f32),
                pltpu.VMEM((total, 128), bf),
                pltpu.VMEM((total, width), bf),
                pltpu.VMEM((total, width), bf),
                pltpu.VMEM(egu.shape, bf),
                pltpu.VMEM(edn.shape, bf),
                pltpu.VMEM((total, width), bf),
                pltpu.VMEM((total, width), bf),
                pltpu.VMEM((experts, slots, width), bf),
                pltpu.VMEM((experts, slots, width), bf),
                pltpu.VMEM((experts, slots, 128), bf),
                pltpu.SemaphoreType.DMA((3, experts)),
                pltpu.SemaphoreType.DMA((5, blocks)),
            ],
        ),
        out_shape=[shape, shape],
        name="experts",
        compiler_params=pltpu.CompilerParams(vmem_limit_bytes=62 << 20),
    )(starts, place_row, place_col, weight_col, rows, grads, egu, edn)


MESH = pl.DeviceIdType.MESH


def place_of():
    return lax.axis_index("fsdp"), lax.axis_index("context"), lax.axis_index("tensor")


def greet(devices):
    barrier = pltpu.get_barrier_semaphore()
    for device in devices:
        pl.semaphore_signal(barrier, inc=1, device_id=device, device_id_type=MESH)
    pl.semaphore_wait(barrier, len(devices))


def send(source, target, send_sem, recv_sem, device):
    return pltpu.make_async_remote_copy(
        src_ref=source,
        dst_ref=target,
        send_sem=send_sem,
        recv_sem=recv_sem,
        device_id=device,
        device_id_type=MESH,
    )


def flip(index, bit):
    return index + (1 - 2 * lax.rem(index // (1 << bit), 2)) * (1 << bit)


def split_rows(count):
    first = (count // 2 + 15) // 16 * 16
    return ((0, first), (first, count - first))


class Gather:
    def __init__(self, bits, me, device_of, own, buf, stride, base, count, send_sems, recv_sems):
        self.stages = [[] for _ in range(bits)]
        self.arrived = [[] for _ in range(bits)]
        self.passed = [[] for _ in range(bits)]
        number = 0
        for half, (offset, size) in enumerate(split_rows(count)):
            held = [me]
            for stage in range(bits):
                bit = (stage + half) % bits
                for block in held:
                    rows = self.rows(block * stride + base + offset, size)
                    source = own.at[self.rows(base + offset, size)] if block is me else buf.at[rows]
                    self.passed[stage].append(block is not me)
                    self.stages[stage].append(
                        send(
                            source,
                            buf.at[rows],
                            send_sems.at[number],
                            recv_sems.at[number],
                            device_of(flip(me, bit)),
                        )
                    )
                    self.arrived[stage].append(
                        self.rows(flip(block, bit) * stride + base + offset, size)
                    )
                    number = number + 1
                held = held + [flip(block, bit) for block in held]

    @staticmethod
    def rows(start, size):
        return pl.ds(pl.multiple_of(start, 16), size)

    def start(self, stage):
        if stage == 0:
            for copies, passed in zip(self.stages, self.passed):
                for copy, later in zip(copies, passed):
                    if not later:
                        copy.start()
        else:
            for copy, later in zip(self.stages[stage], self.passed[stage]):
                if later:
                    copy.start()

    def wait(self, stage):
        for copy in self.stages[stage]:
            copy.wait_recv()

    def finish(self):
        for stage in self.stages:
            for copy in stage:
                copy.wait_send()


def turn(values, cosine, sinus):
    lane = lax.broadcasted_iota(jnp.int32, values.shape, 1)
    first = lax.rem(lane, HEAD_DIM) < HEAD_DIM // 2
    swapped = jnp.where(
        first,
        pltpu.roll(values, 128 - HEAD_DIM // 2, 1),
        pltpu.roll(values, HEAD_DIM // 2, 1),
    )
    return values * cosine + swapped * sinus


def two_parts(values):
    high = values.astype(jnp.bfloat16)
    low = (values - high.astype(jnp.float32)).astype(jnp.bfloat16)
    return jnp.concatenate([high, low], axis=1)


def normed(values, gain):
    scale = lax.rsqrt(jnp.mean(values * values, axis=-1, keepdims=True) + epsilon)
    return (values * scale * gain).astype(jnp.bfloat16)


def fill_bias(bias, hot_rows, reach_t, key_start, query_start):
    seen = nn_dot(hot_rows, reach_t)
    keys = key_start + lax.broadcasted_iota(jnp.int32, seen.shape, 0)
    queries = query_start + lax.broadcasted_iota(jnp.int32, seen.shape, 1)
    bias[...] = jnp.where((seen > 0.5) & (keys <= queries), 0.0, masked_score)


def head_half(shape, axis, odd):
    index = lax.broadcasted_iota(jnp.int32, shape, axis)
    return (index >= HEAD_DIM) if odd else (index < HEAD_DIM)


def tree_tables(parents, lengths, turns, context, rows, hot, reach_t, cosine, sinus):
    lane = lax.broadcasted_iota(jnp.int32, (1, 128), 1)
    far = jnp.full((1, 128), 1 << 30, jnp.int32)
    none = jnp.zeros((1, 128), jnp.int32)
    begins, ends, moves = far, far, none
    first, second = none - 1, none - 1
    start = jnp.int32(0)
    for s in range(parents.shape[1]):
        parent = parents[0, s]
        grand = parents[0, parent]
        here = lane == s
        above = jnp.where(parent != s, lengths[0, parent], 0) + jnp.where(
            (grand != s) & (grand != parent), lengths[0, grand], 0
        )
        begins = jnp.where(here, start, begins)
        moves = jnp.where(here, above - start, moves)
        first = jnp.where(here, parent, first)
        second = jnp.where(here, grand, second)
        start = start + lengths[0, s]
        ends = jnp.where(here, start, ends)
    over = lax.broadcasted_iota(jnp.int32, (128, 128), 0)
    under = lax.broadcasted_iota(jnp.int32, (128, 128), 1)
    ancestors = jnp.where((over == under) | (over == first) | (over == second), 1.0, 0.0).astype(
        jnp.bfloat16
    )

    def fill(chunk, carry):
        block = pl.ds(pl.multiple_of(chunk * rows, 16), rows)
        row = chunk * rows + lax.broadcasted_iota(jnp.int32, (rows, 128), 0)
        inside = (row >= begins) & (row < ends)
        hot[block, :] = jnp.where(inside, 1.0, 0.0).astype(jnp.bfloat16)
        moved = jnp.sum(jnp.where(inside, moves.astype(jnp.float32), 0.0), axis=1, keepdims=True)
        angle = (row.astype(jnp.float32) + moved) * turns[0:1, :]
        cosine[block, :] = jnp.cos(angle)
        sinus[block, :] = jnp.sin(angle) * turns[1:2, :]
        return carry

    lax.fori_loop(0, context + 1, fill, 0)
    own = pl.ds(pl.multiple_of(context * rows, 16), rows)
    reach_t[...] = nt_dot(ancestors, hot[own, :]).astype(jnp.bfloat16)


def choose(ids, adapters_all, out):
    wanted = ids[0]
    own = ADAPTERS // adapters_all.shape[0]
    count = adapters_all.shape[1] // own
    total = jnp.zeros((count, 128), jnp.float32)
    for a in range(ADAPTERS):
        block = adapters_all[a // own, pl.ds((a % own) * count, count), :].astype(jnp.float32)
        total = total + jnp.where(wanted == a, block, 0.0)
    out[...] = total.astype(jnp.bfloat16)


def route_tables(f, table_all, place_row, place_col, weight_col, marks):
    fsdp, _, rows = table_all.shape
    own = EXPERTS // fsdp
    f32 = jnp.float32
    sub = lax.broadcasted_iota(jnp.int32, (8, rows), 0)
    expert = jnp.where(sub < own, f * own + sub, -1).astype(f32)
    before = lax.broadcasted_iota(jnp.int32, (rows, rows), 0)
    after = lax.broadcasted_iota(jnp.int32, (rows, rows), 1)
    upto = jnp.where(before <= after, 1.0, 0.0).astype(jnp.bfloat16)
    lane = lax.broadcasted_iota(jnp.int32, (8, 128), 1)
    base = jnp.zeros((8, 1), f32)
    found = jnp.zeros((8, 128), f32)
    more = jnp.zeros((120, rows), f32)
    for source in range(fsdp):
        table = table_all[source]
        one = table[0:1, :] == expert
        two = table[1:2, :] == expert
        hit = one | two
        weight = jnp.where(one, table[2:3, :], 0.0) + jnp.where(two, table[3:4, :], 0.0)
        count = nn_dot(jnp.where(hit, 1.0, 0.0).astype(jnp.bfloat16), upto) + base
        place = jnp.where(hit, count - 1.0, -1.0)
        block = slice(source * rows, (source + 1) * rows)
        place_row[:, block] = place
        place_col[block, :] = jnp.concatenate([place, more], axis=0).T
        weight_col[block, :] = jnp.concatenate([weight, more], axis=0).T.astype(jnp.bfloat16)
        for token in range(TOKEN_TILE - 1, fsdp * rows, TOKEN_TILE):
            if token // rows == source:
                at = token % rows
                found = jnp.where(lane == token // TOKEN_TILE + 1, count[:, at : at + 1], found)
        base = count[:, rows - 1 : rows]
    marks[...] = found


def unpack_adapter(t, per_block, chosen, flat, wide, first, second):
    a_qkv, b_qkv2, a_qkv_t2, a_o, b_o2, a_o_t2 = first
    a_gu, b_gu2, a_gu_t2, a_dn, a_dn_t2, b_dn2 = second
    f32, bf = jnp.float32, jnp.bfloat16
    contexts = chosen.shape[1]
    width, units = a_o.shape[0], a_dn.shape[0]
    count = PARAMS // 128 // (2 * contexts)
    for context in range(contexts):
        for part in range(2):
            start = (2 * context + part) * count
            flat[start : start + count, :] = chosen[part, context, 0:count, :].astype(f32)

    def spread(start, groups, rank, out, out_t):
        total = groups * 128 // rank
        wide[...] = jnp.zeros_like(wide)
        lines = rank // math.gcd(rank, 128)
        each = lines * 128 // rank
        for i in range(each):
            row, at = divmod(i * rank, 128)
            def line(number):
                if lines == 1:
                    return flat[pl.ds(start, groups), :]
                return flat[pl.ds(start + number, groups // lines, stride=lines), :]

            piece = line(row)[:, at : min(at + rank, 128)]
            if at + rank > 128:
                piece = jnp.concatenate([piece, line(row + 1)[:, 0 : at + rank - 128]], axis=1)
            wide[pl.ds(i, groups // lines, stride=each), 0:rank] = piece
        out[...] = wide[0:total, :].astype(bf)
        if out_t is not None:
            for p in range(total // 128):
                turned = wide[128 * p : 128 * p + 128, :].T.astype(bf)
                out_t[0:128, 128 * p : 128 * p + 128] = turned
                out_t[128:256, 128 * p : 128 * p + 128] = turned

    def stack(start, lines, columns, out, row, column):
        for p, m in enumerate(columns):
            piece = (2.0 * flat[pl.ds(start + m, RANK, stride=lines), :]).astype(bf)
            lanes = slice(column + 128 * p, column + 128 * p + 128)
            out[row : row + RANK, lanes] = piece
            out[128 + row : 128 + row + RANK, lanes] = piece

    for ref in (b_qkv2, b_o2, b_gu2, b_dn2):
        ref[...] = jnp.zeros_like(ref)
    at = 0
    spread(at, 3 * RANK * D // 128, 3 * RANK, a_qkv, a_qkv_t2)
    at = at + 3 * RANK * D // 128
    lines = D // 128
    mine = [t * (width // 128) + p for p in range(width // 128)]
    for j in range(3):
        stack(at + j * RANK * lines, lines, mine, b_qkv2, j * RANK, j * width)
    at = at + 3 * RANK * lines
    spread(at + t * (width * RANK // 128), width * RANK // 128, RANK, a_o, a_o_t2)
    at = at + D * RANK // 128
    stack(at, lines, list(range(lines)), b_o2, 0, 0)
    at = at + RANK * lines
    spread(at, 2 * RANK * D // 128, 2 * RANK, a_gu, a_gu_t2)
    at = at + 2 * RANK * D // 128
    wide_lines = FF // 128
    mine = [t * (units // 128) + p for p in range(units // 128)]
    for j in range(2):
        stack(at + j * RANK * wide_lines, wide_lines, mine, b_gu2, j * RANK, j * units)
    at = at + 2 * RANK * wide_lines
    spread(at + t * (units * RANK // 128), units * RANK // 128, RANK, a_dn, a_dn_t2)
    at = at + FF * RANK // 128
    stack(at, lines, list(range(lines)), b_dn2, 0, 0)


def forward_kernel(
    sizes,
    x_in,
    g_in,
    wq_in,
    wo_in,
    gu_in,
    dn_in,
    adapters_in,
    gains_in,
    table_in,
    turns,
    ids,
    parents,
    lengths,
    n1_all,
    k_all,
    v_all,
    wq_all,
    wo_all,
    n2_all,
    g_all,
    p_all,
    q_t_out,
    q_n_out,
    mixed_out,
    o_t_out,
    lse_out,
    resid_out,
    shared_out,
    dn2_out,
    da_gu,
    db_gu,
    da_dn,
    db_dn,
    gains_out,
    cosine_out,
    sinus_out,
    hot_out,
    reach_t_out,
    a_qkv_out,
    b_qkv2_out,
    a_qkv_t2_out,
    a_o_out,
    b_o2_out,
    a_o_t2_out,
    table_all_out,
    place_row_out,
    place_col_out,
    weight_col_out,
    marks,
    peaks,
    x_buf,
    wq,
    wo,
    gu,
    dn,
    g_own,
    n1_buf,
    k_buf,
    v_buf,
    v_t,
    peak,
    total,
    bias,
    part_out,
    part_in,
    n2_own,
    shared,
    dn2,
    adapters_all,
    gains_all,
    chosen,
    flat,
    a_wide,
    a_gu,
    b_gu2,
    a_gu_t2,
    a_dn,
    a_dn_t2,
    b_dn2,
    fs_send,
    fs_recv,
    z_send,
    z_recv,
    core_send,
    core_recv,
    local_sems,
    chunk_sems,
    small_send,
    small_recv,
    lend_send,
    lend_recv,
    q_t,
    q_n,
    mixed,
    o_t,
    lse,
    resid,
    gains,
    cosine,
    sinus,
    hot,
    reach_t,
    a_qkv,
    b_qkv2,
    a_qkv_t2,
    a_o,
    b_o2,
    a_o_t2,
    table_all,
    place_row,
    place_col,
    weight_col,
    out_sems,
    p_buf,
    p_sems,
):
    fsdp, contexts, _ = sizes
    bits = fsdp.bit_length() - 1
    f, c, t = place_of()
    rows = x_in.shape[0]
    half = rows // 2
    heads = q_t.shape[0] // HEAD_DIM
    width = q_t.shape[0]
    units = dn_in.shape[1]
    own_n = wq_in.shape[0]
    sibling = (f, c, 1 - t)

    def peer(index):
        return (index, c, t)

    peers = [(lax.rem(f + k, fsdp), c, t) for k in range(1, fsdp)]
    stacked = [(f, lax.rem(c + k, contexts), t) for k in range(1, contexts)]
    greet(peers + stacked + [sibling])

    targets = (
        (q_t, q_t_out),
        (q_n, q_n_out),
        (mixed, mixed_out),
        (o_t, o_t_out),
        (lse, lse_out),
        (resid, resid_out),
        (shared, shared_out),
        (dn2, dn2_out),
        (gains, gains_out),
        (cosine, cosine_out),
        (sinus, sinus_out),
        (hot, hot_out),
        (reach_t, reach_t_out),
        (a_qkv, a_qkv_out),
        (b_qkv2, b_qkv2_out),
        (a_qkv_t2, a_qkv_t2_out),
        (a_o, a_o_out),
        (b_o2, b_o2_out),
        (a_o_t2, a_o_t2_out),
        (table_all, table_all_out),
        (place_row, place_row_out),
        (place_col, place_col_out),
        (weight_col, weight_col_out),
    )
    given = []

    def give_out(refs):
        for i, (ref, target) in enumerate(targets):
            if any(ref is other for other in refs):
                copy = pltpu.make_async_copy(ref, target, out_sems.at[i])
                copy.start()
                given.append(copy)

    def half_rows(chunk, part):
        return pl.ds(pl.multiple_of(chunk * rows + part * half, 16), half)

    def up(chunk, source):
        return send(
            source,
            x_buf.at[half_rows(chunk, t)],
            z_send.at[chunk],
            z_recv.at[chunk],
            (f, c + 1, t),
        )

    def across(chunk):
        block = x_buf.at[half_rows(chunk, t)]
        return send(block, block, core_send.at[chunk], core_recv.at[chunk], sibling)

    @pl.when(c < contexts - 1)
    def _():
        up(c, x_in.at[half_rows(0, t)]).start()

    gathers = []
    halved = (False, False, True, False)
    neighbour = (f, c + 1 - 2 * lax.rem(c, 2), t)
    own_half = own_n // 2
    for i, (own, buf) in enumerate(((wq_in, wq), (wo_in, wo), (gu_in, gu), (dn_in, dn))):
        base, count = (lax.rem(c, 2) * own_half, own_half) if halved[i] else (0, own_n)
        gathers.append(
            Gather(bits, f, peer, own, buf, own_n, base, count, fs_send.at[i], fs_recv.at[i])
        )

    def lent(gather, buf, which):
        copies, number = [], 0
        for stage in range(bits):
            group = []
            for block in gather.arrived[stage]:
                group.append(
                    send(
                        buf.at[block],
                        buf.at[block],
                        lend_send.at[which, number],
                        lend_recv.at[which, number],
                        neighbour,
                    )
                )
                number = number + 1
            copies.append(group)
        return copies

    gu_lent = lent(gathers[2], gu, 0)

    z_busy = (lax.rem(c, 2) == 0) & (c > 0)

    def lend(copies, stage):
        for copy in copies[stage]:
            copy.start()
    g_gather = Gather(
        bits, f, peer, g_in, g_all, rows, t * half, half, fs_send.at[4], fs_recv.at[4]
    )
    n2_gather = Gather(
        bits, f, peer, n2_own, n2_all, rows, t * half, half, fs_send.at[5], fs_recv.at[5]
    )
    wq_gather, wo_gather, gu_gather, dn_gather = gathers
    small = []
    for k, other in enumerate(peers):
        for j, (source, target) in enumerate(
            ((adapters_in, adapters_all), (gains_in, gains_all), (table_in, table_all))
        ):
            copy = send(source, target.at[f], small_send.at[j, k], small_recv.at[j, k], other)
            copy.start()
            small.append(copy)
    wq_gather.start(0)
    locals_ = [pltpu.make_async_copy(x_in, x_buf.at[pl.ds(c * rows, rows)], local_sems.at[0])]
    for i, (own, buf) in enumerate(((wq_in, wq), (wo_in, wo), (gu_in, gu), (dn_in, dn))):
        locals_.append(
            pltpu.make_async_copy(own, buf.at[pl.ds(f * own_n, own_n)], local_sems.at[1 + i])
        )
    locals_.append(pltpu.make_async_copy(g_in, g_own, local_sems.at[5]))
    locals_.append(
        pltpu.make_async_copy(g_in, g_all.at[pl.ds(f * rows, rows)], local_sems.at[6])
    )
    for copy in locals_:
        copy.start()

    o_t[...] = jnp.zeros_like(o_t)
    peak[...] = jnp.full_like(peak, masked_score)
    total[...] = jnp.zeros_like(total)
    da_gu[...] = jnp.zeros_like(da_gu)
    db_gu[...] = jnp.zeros_like(db_gu)
    da_dn[...] = jnp.zeros_like(da_dn)
    db_dn[...] = jnp.zeros_like(db_dn)
    adapters_all[f] = adapters_in[...]
    gains_all[f] = gains_in[...]
    table_all[f] = table_in[...]
    tree_tables(parents, lengths, turns, c, rows, hot, reach_t, cosine, sinus)

    def receive(step):
        chunk = c - step

        @pl.when(step <= c)
        def _():
            up(chunk, x_buf.at[half_rows(chunk, t)]).wait_recv()

            @pl.when(c < contexts - 1)
            def _():
                up(chunk, x_buf.at[half_rows(chunk, t)]).start()

            across(chunk).start()

    def chunk_rows(chunk):
        return pl.ds(pl.multiple_of(chunk * rows, 16), rows)

    def out_copies(chunk):
        block = chunk_rows(chunk)
        return [
            pltpu.make_async_copy(n1_buf.at[block], n1_all.at[block], chunk_sems.at[0, chunk]),
            pltpu.make_async_copy(k_buf.at[block], k_all.at[block], chunk_sems.at[1, chunk]),
            pltpu.make_async_copy(v_buf.at[block], v_all.at[block], chunk_sems.at[2, chunk]),
        ]

    def project(chunk, own):
        block = chunk_rows(chunk)
        n1 = normed(x_buf[block, :].astype(jnp.float32), gain_one)
        n1_buf[block, :] = n1
        rank = two_parts(nn_dot(n1, a_qkv[...]))
        cos_rows = cosine[block, :]
        sin_rows = sinus[block, :]
        start = 0 if own else width
        result = nn_dot(n1, wq[:, start:]) + nn_dot(rank, b_qkv2[:, start:])
        for p in range(width // 128):
            lanes = slice(128 * p, 128 * p + 128)
            cols = slice(width - start + 128 * p, width - start + 128 * p + 128)
            k_buf[block, lanes] = turn(result[:, cols], cos_rows, sin_rows).astype(jnp.bfloat16)
            cols = slice(2 * width - start + 128 * p, 2 * width - start + 128 * p + 128)
            value = result[:, cols]
            v_buf[block, lanes] = value.astype(jnp.bfloat16)
            v_t[lanes, :] = value.T.astype(jnp.bfloat16)
            if own:
                query = turn(result[:, lanes], cos_rows, sin_rows) * 0.125
                q_n[:, lanes] = query.astype(jnp.bfloat16)
                q_t[lanes, :] = query.T.astype(jnp.bfloat16)
        for copy in out_copies(chunk):
            copy.start()

    def weights_out(chunk, p):
        target = p_all.at[pl.ds(chunk * heads + 2 * p, 2)]
        return pltpu.make_async_copy(p_buf.at[pl.ds(2 * p, 2)], target, p_sems.at[p])

    def attend(chunk, first):
        block = chunk_rows(chunk)
        fill_bias(bias, hot[block, :], reach_t[...], chunk * rows, c * rows)

        def pair_step(p, carry):
            lanes = pl.ds(pl.multiple_of(p * 128, 128), 128)
            keys = k_buf[block, lanes]
            query = q_t[lanes, :]
            if not first:
                weights_out(chunk, p).wait()
            for odd in range(2):
                h = 2 * p + odd
                alone = jnp.where(
                    head_half(query.shape, 0, odd), query, jnp.zeros_like(query)
                )
                scores = nn_dot(keys, alone) + bias[...]
                before = peak[pl.ds(h, 1), :]
                now = jnp.maximum(before, jnp.max(scores, axis=0, keepdims=True))
                weights = jnp.exp(scores - now)
                shrink = jnp.exp(before - now)
                peak[pl.ds(h, 1), :] = now
                peaks[pl.ds(chunk * 8 + h, 1), :] = now
                low_weights = weights.astype(jnp.bfloat16)
                p_buf[h] = low_weights
                total[pl.ds(h, 1), :] = total[pl.ds(h, 1), :] * shrink + jnp.sum(
                    weights, axis=0, keepdims=True
                )
                head = pl.ds(pl.multiple_of(h * HEAD_DIM, HEAD_DIM), HEAD_DIM)
                o_t[head, :] = o_t[head, :] * shrink + nn_dot(
                    v_t[head, :], low_weights
                )
            weights_out(chunk, p).start()
            return carry

        lax.fori_loop(0, heads // 2, pair_step, 0)

    def advance(gather, following, copies=None):
        gather.wait(0)
        for stage in range(1, bits):
            gather.start(stage)
            if copies is not None:
                lend(copies, stage - 1)
            if stage < bits - 1:
                gather.wait(stage)
        following.start(0)

    for copy in small:
        copy.wait_recv()
    choose(ids, adapters_all, chosen.at[t, c])
    spread = []
    for k, other in enumerate(stacked):
        block = chosen.at[t, c]
        copy = send(block, block, small_send.at[3, k], small_recv.at[3, k], other)
        copy.start()
        spread.append(copy)
    gains[...] = jnp.zeros_like(gains)
    for i in range(2):
        pieces = [
            gains_all[b, 0:1, i * own_n : (i + 1) * own_n].astype(jnp.float32)
            for b in range(fsdp)
        ]
        gains[i : i + 1, :] = jnp.concatenate(pieces, axis=1)
    gain_one = gains[0:1, :]
    gain_two = gains[1:2, :]
    advance(wq_gather, wo_gather)
    receive(1)
    for copy in spread:
        copy.wait_recv()
    shared_copy = send(
        chosen.at[t], chosen.at[t], small_send.at[4, 0], small_recv.at[4, 0], sibling
    )
    shared_copy.start()
    route_tables(f, table_all, place_row, place_col, weight_col, marks)
    give_out(
        (table_all, place_row, place_col, weight_col, gains, cosine, sinus, hot, reach_t)
    )
    advance(wo_gather, gu_gather)
    shared_copy.wait_recv()
    unpack_adapter(
        t,
        adapters_in.shape[0] // (ADAPTERS // fsdp),
        chosen,
        flat,
        a_wide,
        (a_qkv, b_qkv2, a_qkv_t2, a_o, b_o2, a_o_t2),
        (a_gu, b_gu2, a_gu_t2, a_dn, a_dn_t2, b_dn2),
    )
    give_out((a_qkv, b_qkv2, a_qkv_t2, a_o, b_o2, a_o_t2))
    wq_gather.wait(bits - 1)
    locals_[0].wait()
    locals_[1].wait()
    wq_out = pltpu.make_async_copy(wq, wq_all, local_sems.at[10])
    wq_out.start()
    project(c, True)
    receive(2)
    attend(c, True)

    number = contexts

    def forwards(gather, buf, first):
        copies = []
        for stage in range(bits):
            group = []
            for block in gather.arrived[stage]:
                index = first + len(copies)
                copies.append(
                    send(
                        buf.at[block],
                        buf.at[block],
                        core_send.at[index],
                        core_recv.at[index],
                        sibling,
                    )
                )
        return copies

    per_stage = [len(stage) for stage in g_gather.arrived]
    g_forward = forwards(g_gather, g_all, number + 5)
    n2_forward = forwards(n2_gather, n2_all, number + 5 + sum(per_stage))

    def pass_on(copies, stage):
        start = sum(per_stage[:stage])
        for copy in copies[start : start + per_stage[stage]]:
            copy.start()

    def between(step):
        if step == 1:
            advance(gu_gather, dn_gather)

            @pl.when(jnp.logical_not(z_busy))
            def _():
                lend(gu_lent, 0)

        if step == 2:
            advance(dn_gather, g_gather)
            gu_gather.wait(bits - 1)

            @pl.when(z_busy)
            def _():
                lend(gu_lent, 0)

            for stage in range(1, bits):
                lend(gu_lent, stage)
        if step == 3:
            g_gather.wait(0)
            for stage in range(1, bits):
                g_gather.start(stage)
                pass_on(g_forward, stage - 1)
                if stage < bits - 1:
                    g_gather.wait(stage)

    def later(step):
        chunk = c - step

        @pl.when(step <= c)
        def _():
            across(chunk).wait_recv()
            project(chunk, False)
            receive(step + 2)
            attend(chunk, False)

    for step in range(1, 3):
        between(step)
        later(step)

    @pl.when(c >= 3)
    def _():
        between(3)
        later(3)

    def rest(step, carry):
        later(step)
        return carry

    lax.fori_loop(4, contexts, rest, 0)

    for h in range(heads):
        head = slice(h * HEAD_DIM, h * HEAD_DIM + HEAD_DIM)
        o_t[head, :] = o_t[head, :] / total[h : h + 1, :]
    lse[...] = peak[...] + jnp.log(total[...])
    for p in range(width // 128):
        mixed[:, 128 * p : 128 * p + 128] = o_t[128 * p : 128 * p + 128, :].T.astype(jnp.bfloat16)
    give_out((q_t, q_n, mixed, o_t, lse))
    wo_gather.wait(bits - 1)
    locals_[2].wait()
    wo_out = pltpu.make_async_copy(wo, wo_all, local_sems.at[11])
    wo_out.start()

    def local_rows(part):
        return pl.ds(pl.multiple_of(part * half, 16), half)

    mine = local_rows(t)
    theirs = local_rows(1 - t)

    def branch(block):
        values = mixed[block, :]
        rank = two_parts(nn_dot(values, a_o[...]))
        return nt_dot(values, wo[...]) + nn_dot(rank, b_o2[...])

    part_copies = []
    for i, block in enumerate((theirs, mine)):
        part_out[block, :] = branch(block).astype(jnp.bfloat16)
        copy = send(
            part_out.at[block],
            part_in.at[block],
            core_send.at[number + i],
            core_recv.at[number + i],
            sibling,
        )
        copy.start()
        part_copies.append(copy)

    def attended(block, copy):
        copy.wait_recv()
        resid[block, :] = x_rows(x_buf, c, rows, block) + (
            part_out[block, :].astype(jnp.float32) + part_in[block, :].astype(jnp.float32)
        )
        n2_own[block, :] = normed(resid[block, :], gain_two)

    attended(mine, part_copies[0])
    n2_gather.start(0)
    attended(theirs, part_copies[1])
    give_out((resid,))
    n2_out = pltpu.make_async_copy(n2_own, n2_all.at[pl.ds(f * rows, rows)], local_sems.at[12])
    n2_out.start()

    @pl.when(c < 3)
    def _():
        between(3)


    locals_[5].wait()
    for group in gu_lent:
        for copy in group:
            copy.wait_recv()
    locals_[3].wait()
    dn_gather.wait(bits - 1)
    locals_[4].wait()

    def shared_tile(block):
        inputs = n2_own[block, :]
        grads = g_own[block, :]
        rank = nn_dot(inputs, a_gu[...])
        rank2 = two_parts(rank)
        gate = nn_dot(inputs, gu[:, :units]) + nn_dot(rank2, b_gu2[:, :units])
        up_pre = nn_dot(inputs, gu[:, units:]) + nn_dot(rank2, b_gu2[:, units:])
        sigmoid_gate = jax.nn.sigmoid(gate)
        silu = gate * sigmoid_gate
        hidden = (silu * up_pre).astype(jnp.bfloat16)
        down_rank = nn_dot(hidden, a_dn[...])
        shared[block, :] = (
            nt_dot(hidden, dn[...]) + nn_dot(two_parts(down_rank), b_dn2[...])
        ).astype(jnp.bfloat16)
        down_back = nt_dot(grads, b_dn2[0:128, :])
        grad_hidden = nn_dot(grads, dn[...]) + nn_dot(two_parts(down_back), a_dn_t2[...])
        grad_gate = (
            grad_hidden * up_pre * sigmoid_gate * (1.0 + gate * (1.0 - sigmoid_gate))
        ).astype(jnp.bfloat16)
        grad_up = (grad_hidden * silu).astype(jnp.bfloat16)
        rank_back = nt_dot(grad_gate, b_gu2[0:128, :units]) + nt_dot(
            grad_up, b_gu2[0:128, units:]
        )
        dn2[block, :] = (
            nt_dot(grad_gate, gu[:, :units])
            + nt_dot(grad_up, gu[:, units:])
            + nn_dot(two_parts(rank_back), a_gu_t2[...])
        ).astype(jnp.bfloat16)
        rank_low = rank.astype(jnp.bfloat16)
        da_gu[...] += tn_dot(rank_back.astype(jnp.bfloat16), inputs)[0 : 2 * RANK]
        db_gu[0:RANK, :] += 2.0 * tn_dot(rank_low, grad_gate)[0:RANK]
        db_gu[RANK:, :] += 2.0 * tn_dot(rank_low, grad_up)[RANK : 2 * RANK]
        da_dn[...] += tn_dot(down_back.astype(jnp.bfloat16), hidden)[0:RANK]
        db_dn[...] += 2.0 * tn_dot(down_rank.astype(jnp.bfloat16), grads)[0:RANK]

    def pass_pieces(gather, copies, stage):
        start = sum(per_stage[:stage])
        for i, copy in enumerate(gather.stages[stage]):
            copy.wait_recv()
            copies[start + i].start()

    shared_tile(mine)
    n2_gather.wait(0)
    for stage in range(1, bits):
        n2_gather.start(stage)
        pass_on(n2_forward, stage - 1)
        if stage < bits - 1:
            n2_gather.wait(stage)
    shared_tile(theirs)
    give_out((shared, dn2))
    pass_pieces(g_gather, g_forward, bits - 1)
    pass_pieces(n2_gather, n2_forward, bits - 1)
    for copy in n2_forward + g_forward:
        copy.wait()
    for copy in small + spread + [shared_copy]:
        copy.wait_send()
    for group in gu_lent:
        for copy in group:
            copy.wait_send()
    for copy in given:
        copy.wait()
    for copy in part_copies:
        copy.wait_send()
    for gather in gathers + [g_gather, n2_gather]:
        gather.finish()
    n2_out.wait()
    wq_out.wait()
    wo_out.wait()
    locals_[6].wait()

    @pl.when(c < contexts - 1)
    def _():
        up(c, x_in.at[half_rows(0, t)]).wait_send()

    def drain(step, carry):
        chunk = c - step

        @pl.when(c < contexts - 1)
        def _():
            up(chunk, x_buf.at[half_rows(chunk, t)]).wait_send()

        across(chunk).wait_send()
        return carry

    lax.fori_loop(1, c + 1, drain, 0)

    def drain_out(step, carry):
        for copy in out_copies(c - step):
            copy.wait()
        return carry

    lax.fori_loop(0, c + 1, drain_out, 0)
    for p in range(heads // 2):
        weights_out(0, p).wait()


def x_rows(x_buf, chunk, rows, block):
    return x_buf[pl.ds(pl.multiple_of(chunk * rows, 16) + block.start, block.size), :].astype(
        jnp.float32
    )


def forward_call(sizes, sharded, local):
    fsdp, contexts, _ = sizes
    x, g, wq, wo, gu, dn = sharded
    adapters, gains, table = local[:3]
    rows = x.shape[0]
    tree = rows * contexts
    width = wo.shape[1]
    units = dn.shape[1]
    bf, f32 = jnp.bfloat16, jnp.float32
    vmem = pl.BlockSpec(memory_space=pltpu.VMEM)
    hbm = pl.BlockSpec(memory_space=pl.ANY)
    smem = pl.BlockSpec(memory_space=pltpu.SMEM)
    slots = max(fsdp, contexts)
    total = fsdp * rows
    per_adapter = adapters.shape[0] // (ADAPTERS // fsdp)

    def shape(kind, *dims):
        return jax.ShapeDtypeStruct(dims, kind)

    moves = 2 * (fsdp - 1)
    hops = contexts + 5 + 2 * moves
    return pl.pallas_call(
        functools.partial(forward_kernel, sizes),
        in_specs=[hbm] * 6 + [vmem] * 4 + [smem] * 3,
        out_specs=[hbm] * 8 + [hbm, hbm, hbm, hbm, hbm, hbm, hbm, hbm, vmem, vmem, vmem, vmem, hbm, hbm, hbm, hbm, hbm, hbm, hbm, hbm, hbm, hbm, hbm, hbm, hbm, hbm, hbm, vmem, vmem],
        out_shape=[
            shape(bf, tree, D),
            shape(bf, tree, width),
            shape(bf, tree, width),
            shape(bf, D, 3 * width),
            shape(bf, D, width),
            shape(bf, fsdp * rows, D),
            shape(bf, fsdp * rows, D),
            shape(bf, contexts * (width // HEAD_DIM), rows, rows),
            shape(bf, width, rows),
            shape(bf, rows, width),
            shape(bf, rows, width),
            shape(f32, width, rows),
            shape(f32, 8, rows),
            shape(f32, rows, D),
            shape(bf, rows, D),
            shape(bf, rows, D),
            shape(f32, 2 * RANK, D),
            shape(f32, 2 * RANK, units),
            shape(f32, RANK, units),
            shape(f32, RANK, D),
            shape(f32, 8, D),
            shape(f32, tree, 128),
            shape(f32, tree, 128),
            shape(bf, tree, 128),
            shape(bf, 128, rows),
            shape(bf, D, 128),
            shape(bf, 256, 3 * width),
            shape(bf, 256, D),
            shape(bf, width, 128),
            shape(bf, 256, D),
            shape(bf, 256, width),
            shape(f32, fsdp, 8, rows),
            shape(f32, 8, total),
            shape(f32, total, 128),
            shape(bf, total, 128),
            shape(f32, 8, 128),
            shape(f32, contexts * 8, rows),
        ],
        scratch_shapes=[
            pltpu.VMEM((tree, D), bf),
            pltpu.VMEM((D, 3 * width), bf),
            pltpu.VMEM((D, width), bf),
            pltpu.VMEM((D, 2 * units), bf),
            pltpu.VMEM((D, units), bf),
            pltpu.VMEM((rows, D), bf),
            pltpu.VMEM((tree, D), bf),
            pltpu.VMEM((tree, width), bf),
            pltpu.VMEM((tree, width), bf),
            pltpu.VMEM((width, rows), bf),
            pltpu.VMEM((8, rows), f32),
            pltpu.VMEM((8, rows), f32),
            pltpu.VMEM((rows, rows), f32),
            pltpu.VMEM((rows, D), bf),
            pltpu.VMEM((rows, D), bf),
            pltpu.VMEM((rows, D), bf),
            pltpu.VMEM((rows, D), bf),
            pltpu.VMEM((rows, D), bf),
            pltpu.VMEM((fsdp,) + adapters.shape, bf),
            pltpu.VMEM((fsdp,) + gains.shape, bf),
            pltpu.VMEM((2, contexts, per_adapter, 128), bf),
            pltpu.VMEM((PARAMS // 128, 128), f32),
            pltpu.VMEM((max(D, units), 128), f32),
            pltpu.VMEM((D, 128), bf),
            pltpu.VMEM((256, 2 * units), bf),
            pltpu.VMEM((256, D), bf),
            pltpu.VMEM((units, 128), bf),
            pltpu.VMEM((256, units), bf),
            pltpu.VMEM((256, D), bf),
            pltpu.SemaphoreType.DMA((6, moves)),
            pltpu.SemaphoreType.DMA((6, moves)),
            pltpu.SemaphoreType.DMA((contexts,)),
            pltpu.SemaphoreType.DMA((contexts,)),
            pltpu.SemaphoreType.DMA((hops,)),
            pltpu.SemaphoreType.DMA((hops,)),
            pltpu.SemaphoreType.DMA((13,)),
            pltpu.SemaphoreType.DMA((3, contexts)),
            pltpu.SemaphoreType.DMA((5, slots)),
            pltpu.SemaphoreType.DMA((5, slots)),
            pltpu.SemaphoreType.DMA((2, moves)),
            pltpu.SemaphoreType.DMA((2, moves)),
            pltpu.VMEM((width, rows), bf),
            pltpu.VMEM((rows, width), bf),
            pltpu.VMEM((rows, width), bf),
            pltpu.VMEM((width, rows), f32),
            pltpu.VMEM((8, rows), f32),
            pltpu.VMEM((rows, D), f32),
            pltpu.VMEM((8, D), f32),
            pltpu.VMEM((tree, 128), f32),
            pltpu.VMEM((tree, 128), f32),
            pltpu.VMEM((tree, 128), bf),
            pltpu.VMEM((128, rows), bf),
            pltpu.VMEM((D, 128), bf),
            pltpu.VMEM((256, 3 * width), bf),
            pltpu.VMEM((256, D), bf),
            pltpu.VMEM((width, 128), bf),
            pltpu.VMEM((256, D), bf),
            pltpu.VMEM((256, width), bf),
            pltpu.VMEM((fsdp, 8, rows), f32),
            pltpu.VMEM((8, total), f32),
            pltpu.VMEM((total, 128), f32),
            pltpu.VMEM((total, 128), bf),
            pltpu.SemaphoreType.DMA((23,)),
            pltpu.VMEM((width // HEAD_DIM, rows, rows), bf),
            pltpu.SemaphoreType.DMA((width // HEAD_DIM // 2,)),
        ],
        name="forward",
        compiler_params=pltpu.CompilerParams(
            collective_id=2, has_side_effects=True, vmem_limit_bytes=62 << 20
        ),
    )(*sharded, *local)


def flips(index, mask, bits):
    for bit in range(bits):
        if mask >> bit & 1:
            index = flip(index, bit)
    return index


class Scatter:
    def __init__(self, bits, me, device_of, work, inbox, count, send_sems, recv_sems):
        self.bits, self.work, self.inbox = bits, work, inbox
        self.copies = [[] for _ in range(bits)]
        self.masks = [[] for _ in range(bits)]
        self.adds = [[] for _ in range(bits)]
        number = 0
        for half, (offset, size) in enumerate(split_rows(count)):
            alive = list(range(1 << bits))
            slot = 0
            for stage in range(bits):
                bit = (stage + half) % bits
                for mask in alive:
                    if mask >> bit & 1:
                        source = Gather.rows(flips(me, mask, bits) * count + offset, size)
                        target = pl.ds(slot * count + offset, size)
                        kept = Gather.rows(flips(me, mask ^ (1 << bit), bits) * count + offset, size)
                        self.copies[stage].append(
                            send(
                                work.at[source],
                                inbox.at[target],
                                send_sems.at[number],
                                recv_sems.at[number],
                                device_of(flip(me, bit)),
                            )
                        )
                        self.adds[stage].append((kept, target, pl.ds(offset, size)))
                        self.masks[stage].append(mask)
                        number = number + 1
                        slot = slot + 1
                alive = [mask for mask in alive if not mask >> bit & 1]

    def start(self, stage):
        for copy in self.copies[stage]:
            copy.start()

    def start_mask(self, mask):
        for copy, number in zip(self.copies[0], self.masks[0]):
            if number == mask:
                copy.start()

    def add(self, stage):
        for copy in self.copies[stage]:
            copy.wait_recv()
        for kept, target, _ in self.adds[stage]:
            total = self.work[kept, :].astype(jnp.float32) + self.inbox[target, :].astype(
                jnp.float32
            )
            self.work[kept, :] = total.astype(jnp.bfloat16)

    def last(self, out):
        for copy in self.copies[self.bits - 1]:
            copy.wait_recv()
        for kept, target, rows in self.adds[self.bits - 1]:
            total = self.work[kept, :].astype(jnp.float32) + self.inbox[target, :].astype(
                jnp.float32
            )
            out[rows, :] = total.astype(jnp.bfloat16)

    def finish(self):
        for stage in self.copies:
            for copy in stage:
                copy.wait_send()


def pack_rows(grad_t, start, rank, flat, wide):
    total = grad_t.shape[1]
    more = jnp.zeros((128 - rank, 128), jnp.float32)
    for p in range(total // 128):
        piece = grad_t[:, 128 * p : 128 * p + 128]
        wide[128 * p : 128 * p + 128, :] = jnp.concatenate([piece, more], axis=0).T
    lines = rank // math.gcd(rank, 128)
    each = lines * 128 // rank
    count = total // each
    joined = jnp.concatenate(
        [wide[pl.ds(i, count, stride=each), :][:, 0:rank] for i in range(each)], axis=1
    )
    if lines == 1:
        flat[pl.ds(start, count), :] = joined
    else:
        for i in range(lines):
            flat[pl.ds(start + i, count, stride=lines), :] = joined[:, 128 * i : 128 * i + 128]


def pack_lines(grad, start, lines, columns, flat):
    for p, m in enumerate(columns):
        flat[pl.ds(start + m, grad.shape[0], stride=lines), :] = grad[:, 128 * p : 128 * p + 128]


def pack_first(t, flat, wide, da_qkv, db_qkv, da_o, db_o):
    width = da_o.shape[1]
    lines = D // 128
    mine = [t * (width // 128) + p for p in range(width // 128)]
    pack_rows(da_qkv[...], 0, 3 * RANK, flat, wide)
    at = 3 * RANK * D // 128
    for j in range(3):
        rows = slice(j * RANK, (j + 1) * RANK)
        pack_lines(db_qkv[rows, :], at + j * RANK * lines, lines, mine, flat)
    at = at + 3 * RANK * lines
    pack_rows(da_o[...], at + t * (width * RANK // 128), RANK, flat, wide)
    at = at + D * RANK // 128
    pack_lines(db_o[...], at, lines, list(range(lines)), flat)


def pack_second(t, flat, wide, da_gu, db_gu, da_dn, db_dn):
    units = da_dn.shape[1]
    lines = D // 128
    at = 8 * RANK * D // 128
    pack_rows(da_gu[...], at, 2 * RANK, flat, wide)
    at = at + 2 * RANK * D // 128
    wide_lines = FF // 128
    mine = [t * (units // 128) + p for p in range(units // 128)]
    for j in range(2):
        rows = slice(j * RANK, (j + 1) * RANK)
        pack_lines(db_gu[rows, :], at + j * RANK * wide_lines, wide_lines, mine, flat)
    at = at + 2 * RANK * wide_lines
    pack_rows(da_dn[...], at + t * (units * RANK // 128), RANK, flat, wide)
    at = at + FF * RANK // 128
    pack_lines(db_dn[...], at, lines, list(range(lines)), flat)


def backward_kernel(
    sizes,
    moe_out,
    moe_back,
    n1_hbm,
    k_hbm,
    v_hbm,
    wq_hbm,
    wo_hbm,
    cos_hbm,
    sin_hbm,
    p_hbm,
    x_in_hbm,
    g_in_hbm,
    gains,
    peaks,
    resid_hbm,
    shared_hbm,
    dn2_hbm,
    q_t_hbm,
    q_n_hbm,
    mixed_hbm,
    o_t_hbm,
    lse,
    a_qkv_hbm,
    b_qkv2_hbm,
    a_qkv_t2_hbm,
    a_o_hbm,
    a_o_t2_hbm,
    b_o2_hbm,
    da_gu,
    db_gu,
    da_dn,
    db_dn,
    table_all,
    block_out,
    input_grad,
    adapter_out,
    cosine,
    sinus,
    k_buf,
    v_buf,
    wq,
    wo,
    work_back,
    pair_back,
    inbox_back,
    work_out,
    pair_out,
    inbox_out,
    total_half,
    total_full,
    ffn_half,
    ffn_full,
    dy,
    do_n,
    do_t,
    delta,
    factor,
    k_t,
    dq_t,
    part_in,
    z_in,
    dn1_full,
    fs_send,
    fs_recv,
    z_send,
    z_recv,
    core_send,
    core_recv,
    pair_send,
    pair_recv,
    local_sems,
    chunk_sems,
    x_in,
    g_in,
    resid,
    shared,
    dn2,
    q_t,
    q_n,
    mixed,
    o_t,
    a_qkv,
    b_qkv2,
    a_qkv_t2,
    a_o,
    a_o_t2,
    b_o2,
    da_qkv,
    db_qkv,
    da_o,
    db_o,
    flat,
    wide,
    packed,
    packed_in,
    up_out,
    up_in,
    own_sum,
    tree_sums,
    in_sems,
    sum_send,
    sum_recv,
    p_buf,
    p_sems,
    whole_back,
    whole_out,
):
    fsdp, contexts, _ = sizes
    bits = fsdp.bit_length() - 1
    f, c, t = place_of()
    rows = x_in.shape[0]
    half = rows // 2
    width = q_t.shape[0]
    inputs = []
    for i, (source, target) in enumerate(
        (
            (x_in_hbm, x_in),
            (g_in_hbm, g_in),
            (resid_hbm, resid),
            (shared_hbm, shared),
            (dn2_hbm, dn2),
            (q_t_hbm, q_t),
            (q_n_hbm, q_n),
            (mixed_hbm, mixed),
            (o_t_hbm, o_t),
            (a_qkv_hbm, a_qkv),
            (b_qkv2_hbm, b_qkv2),
            (a_qkv_t2_hbm, a_qkv_t2),
            (a_o_hbm, a_o),
            (a_o_t2_hbm, a_o_t2),
            (b_o2_hbm, b_o2),
        )
    ):
        inputs.append(pltpu.make_async_copy(source, target, in_sems.at[i]))
    heads = width // HEAD_DIM
    part_out, z_out, grad_kv = pair_back, work_back, inbox_back
    part, n1_buf = whole_back, whole_out
    kv_rows = pl.ds(0, rows)
    sibling = (f, c, 1 - t)
    f32, bf = jnp.float32, jnp.bfloat16

    def peer(index):
        return (index, c, t)

    def local_rows(part_index):
        return pl.ds(pl.multiple_of(part_index * half, 16), half)

    mine = local_rows(t)
    theirs = local_rows(1 - t)

    def block_rows(block, part_index):
        return pl.ds(pl.multiple_of(block * rows + part_index * half, 16), half)

    def work_rows(block):
        return pl.ds(pl.multiple_of(block * half, 16), half)

    masks = list(range(fsdp - 1, -1, -1))

    def exchange(source, work, inbox, which, whole):
        own, sent = [], []
        for mask in masks:
            block = flips(f, mask, bits)
            if mask == 0:
                own.append(
                    pltpu.make_async_copy(
                        source.at[pl.ds(pl.multiple_of(f * rows, 16), rows)],
                        whole,
                        local_sems.at[which, mask],
                    )
                )
                sent.append(
                    send(
                        whole.at[theirs],
                        inbox.at[work_rows(block)],
                        core_send.at[which, mask],
                        core_recv.at[which, mask],
                        sibling,
                    )
                )
                continue
            own.append(
                pltpu.make_async_copy(
                    source.at[block_rows(block, t)],
                    work.at[work_rows(block)],
                    local_sems.at[which, mask],
                )
            )
            sent.append(
                send(
                    source.at[block_rows(block, 1 - t)],
                    inbox.at[work_rows(block)],
                    core_send.at[which, mask],
                    core_recv.at[which, mask],
                    sibling,
                )
            )
        return own, sent

    back_own, back_sent = exchange(moe_back, work_back, pair_back, 0, whole_back)
    out_own, out_sent = exchange(moe_out, work_out, pair_out, 1, whole_out)
    for copy in back_own:
        copy.start()
    wo_copy = pltpu.make_async_copy(wo_hbm, wo, local_sems.at[2, 0])
    wq_copy = pltpu.make_async_copy(wq_hbm, wq, local_sems.at[2, 1])
    wo_copy.start()
    for copy in inputs:
        copy.start()
    peers = [(lax.rem(f + k, fsdp), c, t) for k in range(1, fsdp)]
    stacked = [(f, lax.rem(c + k, contexts), t) for k in range(1, contexts)]
    greet(peers + stacked + [sibling])
    for copy in back_sent[:-1]:
        copy.start()
    for copy in out_own:
        copy.start()
    wq_copy.start()

    lines = PARAMS // 128 // (2 * contexts)
    early = -(-(8 * RANK * D // 128) // (2 * lines))

    def fill_blocks(first, last):
        for context in range(first, last):
            for part_index in range(2):
                start = (2 * context + part_index) * lines
                packed[context, part_index, 0:lines, :] = flat[start : start + lines, :]

    def pair_block(block):
        return send(
            packed.at[block, 1 - t],
            packed_in.at[block],
            sum_send.at[0, block],
            sum_recv.at[0, block],
            sibling,
        )

    def to_owner(k):
        return send(
            up_out.at[k], up_in.at[k], sum_send.at[1, k], sum_recv.at[1, k], stacked[k]
        )

    def push_blocks(soon):
        for k in range(contexts - 1):
            owner = lax.rem(c + k + 1, contexts)

            @pl.when((owner >= early) if soon else (owner < early))
            def _(k=k, owner=owner):
                up_out[k] = (packed[owner, t] + packed_in[owner]).astype(bf)
                to_owner(k).start()

    def to_peer(k):
        return send(
            own_sum, tree_sums.at[k], sum_send.at[2, k], sum_recv.at[2, k], peers[k]
        )

    def sum_own():
        result = packed[c, t] + packed_in[c]
        for k in range(contexts - 1):
            to_owner(k).wait_recv()
            result = result + up_in[k].astype(f32)
        own_sum[...] = result.astype(bf)
        for k in range(fsdp - 1):
            to_peer(k).start()

    def chunk_rows(chunk):
        return pl.ds(pl.multiple_of(chunk * rows, 16), rows)

    def loads(chunk):
        block = chunk_rows(chunk)
        return [
            pltpu.make_async_copy(k_hbm.at[block], k_buf.at[block], chunk_sems.at[1, chunk]),
            pltpu.make_async_copy(v_hbm.at[block], v_buf.at[block], chunk_sems.at[2, chunk]),
        ]

    def n1_load(chunk):
        return pltpu.make_async_copy(
            n1_hbm.at[chunk_rows(chunk)], n1_buf, chunk_sems.at[0, chunk]
        )

    def table_loads(chunk):
        block = chunk_rows(chunk)
        return [
            pltpu.make_async_copy(cos_hbm.at[block], cosine, chunk_sems.at[3, chunk]),
            pltpu.make_async_copy(sin_hbm.at[block], sinus, chunk_sems.at[4, chunk]),
        ]

    def start_loads(chunk, carry):
        for copy in loads(chunk):
            copy.start()
        return carry

    lax.fori_loop(0, c + 1, start_loads, 0)

    def weights_in(chunk, p):
        source = p_hbm.at[pl.ds(chunk * heads + 2 * p, 2)]
        return pltpu.make_async_copy(source, p_buf.at[pl.ds(2 * p, 2)], p_sems.at[p])

    for p in range(heads // 2):
        weights_in(0, p).start()

    back = Scatter(
        bits, f, peer, work_back, inbox_back, half, fs_send.at[0], fs_recv.at[0]
    )
    out = Scatter(bits, f, peer, work_out, inbox_out, half, fs_send.at[1], fs_recv.at[1])

    def join(own, sent, whole, extra, work):
        own[-1].wait()
        whole[...] = (whole[...].astype(f32) + extra[...].astype(f32)).astype(bf)
        sent[-1].start()
        work[work_rows(f), :] = whole[mine, :]

    def pair_sum(own, sent, work, inbox, scatter):
        for i, mask in enumerate(masks):
            block = work_rows(flips(f, mask, bits))
            if mask != 0:
                own[i].wait()
            sent[i].wait_recv()
            work[block, :] = (
                work[block, :].astype(f32) + inbox[block, :].astype(f32)
            ).astype(bf)
            scatter.start_mask(mask)

    for copy in inputs:
        copy.wait()
    join(back_own, back_sent, whole_back, dn2, work_back)
    pair_sum(back_own, back_sent, work_back, pair_back, back)
    for copy in out_sent[:-1]:
        copy.start()
    join(out_own, out_sent, whole_out, shared, work_out)
    flat[...] = jnp.zeros_like(flat)
    pack_second(t, flat, wide, da_gu, db_gu, da_dn, db_dn)
    fill_blocks(early, contexts)
    for block in range(early, contexts):
        pair_block(block).start()
    for stage in range(1, bits):
        back.add(stage - 1)
        back.start(stage)
    dq_t[...] = jnp.zeros_like(dq_t)
    da_qkv[...] = jnp.zeros_like(da_qkv)
    db_qkv[...] = jnp.zeros_like(db_qkv)
    for block in range(early, contexts):
        pair_block(block).wait_recv()
    push_blocks(True)
    back.last(total_half)
    pair_sum(out_own, out_sent, work_out, pair_out, out)
    for copy in out_sent:
        copy.wait_send()
    total_full[mine, :] = total_half[...]
    full_copy = send(
        total_half, total_full.at[mine], core_send.at[2, 0], core_recv.at[2, 0], sibling
    )
    full_copy.start()
    back.finish()
    for copy in back_sent:
        copy.wait_send()
    gain_one = gains[0:1, :]
    gain_two = gains[1:2, :]
    wo_copy.wait()
    full_copy.wait_recv()

    def attn_tile(i, carry):
        block = local_rows(i)
        values = resid[block, :]
        gradient = g_in[block, :].astype(f32) + norm_back(
            values, rms_scale(values), gain_two, total_full[block, :].astype(f32)
        )
        dy[block, :] = gradient
        low_grad = gradient.astype(bf)
        rank_back = nt_dot(low_grad, b_o2[0:128, :])
        do_n[block, :] = (
            nn_dot(low_grad, wo[...]) + nn_dot(two_parts(rank_back), a_o_t2[...])
        ).astype(bf)
        values_o = mixed[block, :]
        rank = nn_dot(values_o, a_o[...])
        first = tn_dot(rank_back.astype(bf), values_o)[0:RANK]
        second = 2.0 * tn_dot(rank.astype(bf), low_grad)[0:RANK]

        @pl.when(i == 0)
        def _():
            da_o[...] = first
            db_o[...] = second

        @pl.when(i > 0)
        def _():
            da_o[...] += first
            db_o[...] += second

        return carry

    lax.fori_loop(0, 2, attn_tile, 0)
    for p in range(width // 128):
        lanes = slice(128 * p, 128 * p + 128)
        turned = do_n[:, lanes].astype(f32).T
        do_t[lanes, :] = turned.astype(bf)
        product = turned * o_t[lanes, :]
        for odd in range(2):
            delta[2 * p + odd : 2 * p + odd + 1, :] = jnp.sum(
                product[HEAD_DIM * odd : HEAD_DIM * odd + HEAD_DIM, :], axis=0, keepdims=True
            )
    wq_copy.wait()

    def attend_back(chunk):
        block = chunk_rows(chunk)
        n1_load(chunk).start()
        for copy in table_loads(chunk):
            copy.start()
        for copy in table_loads(chunk) + loads(chunk):
            copy.wait()
        scale = jnp.exp(peaks[pl.ds(pl.multiple_of(chunk * 8, 8), 8), :] - lse[...])
        factor[...] = scale
        cos_rows = cosine[...]
        sin_rows = -sinus[...]
        for p in range(width // 128):
            lanes = slice(128 * p, 128 * p + 128)
            k_t[lanes, :] = k_buf[block, lanes].astype(f32).T.astype(bf)

        def pair_step(p, carry):
            lanes = pl.ds(pl.multiple_of(p * 128, 128), 128)
            weights_in(chunk, p).wait()
            values = v_buf[block, lanes]
            grad_t = do_t[lanes, :]
            query = q_n[:, lanes]
            grad = do_n[:, lanes]
            grad_keys = jnp.zeros((rows, 128), f32)
            grad_values = jnp.zeros((rows, 128), f32)
            for odd in range(2):
                h = 2 * p + odd
                upper = head_half(grad_t.shape, 0, odd)
                side = head_half(query.shape, 1, odd)
                none_t = jnp.zeros_like(grad_t)
                none = jnp.zeros_like(query)
                weights = p_buf[h].astype(f32) * factor[pl.ds(h, 1), :]
                low_weights = weights.astype(bf)
                grad_weights = nn_dot(values, jnp.where(upper, grad_t, none_t))
                grad_scores = (weights * (grad_weights - delta[pl.ds(h, 1), :])).astype(bf)
                grad_values += nn_dot(low_weights, jnp.where(side, grad, none))
                grad_keys += nn_dot(grad_scores, jnp.where(side, query, none))
                head = pl.ds(pl.multiple_of(h * HEAD_DIM, HEAD_DIM), HEAD_DIM)
                dq_t[head, :] += nn_dot(k_t[head, :], grad_scores)
            grad_kv[kv_rows, lanes] = turn(grad_keys, cos_rows, sin_rows).astype(bf)
            grad_kv[kv_rows, pl.ds(pl.multiple_of(width + p * 128, 128), 128)] = grad_values.astype(bf)

            @pl.when(chunk < c)
            def _():
                weights_in(chunk + 1, p).start()

            return carry

        lax.fori_loop(0, heads // 2, pair_step, 0)

    def project_back(chunk, own):
        block = chunk_rows(chunk)
        grads = grad_kv[kv_rows, :]
        result = nt_dot(grads, wq[:, width:])
        rank_back = nt_dot(grads, b_qkv2[0:128, width:])
        n1_load(chunk).wait()
        n1 = n1_buf[...]
        rank = nn_dot(n1, a_qkv[...]).astype(bf)
        both = 2.0 * tn_dot(rank, grads)
        db_qkv[RANK : 2 * RANK, :] += both[RANK : 2 * RANK, :width]
        db_qkv[2 * RANK :, :] += both[2 * RANK : 3 * RANK, width:]
        if own:
            pieces = []
            for p in range(width // 128):
                lanes = slice(128 * p, 128 * p + 128)
                grad_query = (dq_t[lanes, :] * 0.125).T
                pieces.append(
                    turn(grad_query, cosine[...], -sinus[...]).astype(bf)
                )
            grad_query = jnp.concatenate(pieces, axis=1)
            result += nt_dot(grad_query, wq[:, :width])
            rank_back += nt_dot(grad_query, b_qkv2[0:128, :width])
            db_qkv[0:RANK, :] += 2.0 * tn_dot(rank, grad_query)[0:RANK, :]
        result += nn_dot(two_parts(rank_back), a_qkv_t2[...])
        da_qkv[...] += tn_dot(rank_back.astype(bf), n1)[0 : 3 * RANK]
        part[...] = result.astype(bf)
        part_out[work_rows(chunk), :] = part[theirs, :]
        z_out[work_rows(chunk), :] = part[mine, :]

    def pair_copy(chunk):
        return send(
            part_out.at[work_rows(chunk)],
            part_in.at[work_rows(chunk)],
            pair_send.at[chunk],
            pair_recv.at[chunk],
            sibling,
        )

    def down(chunk):
        block = work_rows(chunk)
        return send(
            z_out.at[block], z_in.at[block], z_send.at[chunk], z_recv.at[chunk], (f, c - 1, t)
        )

    def chain(chunk):
        block = work_rows(chunk)
        pair_copy(chunk).wait_recv()
        summed = z_out[block, :].astype(f32) + part_in[block, :].astype(f32)
        z_out[block, :] = summed.astype(bf)

        @pl.when(c < contexts - 1)
        def _():
            down(chunk).wait_recv()
            z_out[block, :] = (summed + z_in[block, :].astype(f32)).astype(bf)

    def pass_down(chunk):
        chain(chunk)
        down(chunk).start()

    def sum_moe():
        for stage in range(1, bits):
            out.add(stage - 1)
            out.start(stage)

    ffn_copy = send(ffn_half, ffn_full.at[mine], core_send.at[2, 1], core_recv.at[2, 1], sibling)

    def share_moe():
        out.last(ffn_half)
        ffn_full[mine, :] = ffn_half[...]
        ffn_copy.start()

    def step(chunk, carry):
        attend_back(chunk)
        project_back(chunk, False)
        pair_copy(chunk).start()

        @pl.when(c == contexts - 1)
        def _():
            pass_down(chunk)

        @pl.when((c < contexts - 1) & (chunk >= 1))
        def _():
            pass_down(chunk - 1)

        @pl.when(chunk == 0)
        def _():
            sum_moe()

        @pl.when(chunk == 1)
        def _():
            share_moe()

            @pl.when(c >= early)
            def _():
                sum_own()

        return carry

    lax.fori_loop(0, c, step, 0)
    attend_back(c)
    project_back(c, True)
    pair_copy(c).start()
    pack_first(t, flat, wide, da_qkv, db_qkv, da_o, db_o)
    fill_blocks(0, early)
    for block in range(early):
        pair_block(block).start()

    @pl.when((c < 2) & (c >= early))
    def _():
        sum_own()

    @pl.when(c == 0)
    def _():
        sum_moe()

    @pl.when((c < contexts - 1) & (c >= 1))
    def _():
        pass_down(c - 1)

    for block in range(early):
        pair_block(block).wait_recv()
    push_blocks(False)

    @pl.when(c < 2)
    def _():
        share_moe()

    chain(c)
    dn1_full[mine, :] = z_out[work_rows(c), :]
    dn1_copy = send(
        z_out.at[work_rows(c)],
        dn1_full.at[mine],
        core_send.at[2, 2],
        core_recv.at[2, 2],
        sibling,
    )
    dn1_copy.start()
    ffn_copy.wait_recv()
    resid[...] = resid[...] + ffn_full[...].astype(f32)
    block_copy = pltpu.make_async_copy(resid, block_out, in_sems.at[len(inputs)])
    block_copy.start()
    dn1_copy.wait_recv()

    def final_tile(i, carry):
        block = local_rows(i)
        values = x_in[block, :].astype(f32)
        dy[block, :] = dy[block, :] + norm_back(
            values, rms_scale(values), gain_one, dn1_full[block, :].astype(f32)
        )
        return carry

    lax.fori_loop(0, 2, final_tile, 0)
    grad_copy = pltpu.make_async_copy(dy, input_grad, in_sems.at[len(inputs) + 1])
    grad_copy.start()
    @pl.when(c < early)
    def _():
        sum_own()

    own = ADAPTERS // fsdp
    wanted = [(f * own + a).astype(f32) for a in range(own)]
    mine_sum = own_sum[...].astype(f32)
    sums = [jnp.where(table_all[f, 4:5, 0:1] == w, mine_sum, 0.0) for w in wanted]
    for k in range(fsdp - 1):
        to_peer(k).wait_recv()
        tree = table_all[lax.rem(f - k - 1 + fsdp, fsdp), 4:5, 0:1]
        block = tree_sums[k].astype(f32)
        sums = [total + jnp.where(tree == w, block, 0.0) for total, w in zip(sums, wanted)]
    for a in range(own):
        adapter_out[a] = sums[a]
    for copy in [full_copy, ffn_copy, dn1_copy]:
        copy.wait_send()
    block_copy.wait()
    grad_copy.wait()
    for block in range(contexts):
        pair_block(block).wait_send()
    for k in range(contexts - 1):
        to_owner(k).wait_send()
    for k in range(fsdp - 1):
        to_peer(k).wait_send()
    out.finish()

    def drain(chunk, carry):
        pair_copy(chunk).wait_send()

        @pl.when(chunk < c)
        def _():
            down(chunk).wait_send()

        return carry

    lax.fori_loop(0, c + 1, drain, 0)


def backward_call(sizes, remote, local):
    fsdp, contexts, _ = sizes
    rows = local[0].shape[0]
    padded = (PARAMS // 128 // (2 * contexts) + 15) // 16 * 16
    half = rows // 2
    tree = rows * contexts
    width = remote[6].shape[1]
    units = local[19].shape[1]
    bf, f32 = jnp.bfloat16, jnp.float32
    vmem = pl.BlockSpec(memory_space=pltpu.VMEM)
    hbm = pl.BlockSpec(memory_space=pl.ANY)

    def shape(kind, *dims):
        return jax.ShapeDtypeStruct(dims, kind)

    moves = 2 * (fsdp - 1)
    slots = max(fsdp, 4)
    dma = pltpu.SemaphoreType.DMA
    return pl.pallas_call(
        functools.partial(backward_kernel, sizes),
        in_specs=[hbm] * len(remote) + [hbm, hbm, vmem, vmem, hbm, hbm, hbm, hbm, hbm, hbm, hbm, vmem, hbm, hbm, hbm, hbm, hbm, hbm, vmem, vmem, vmem, vmem, vmem],
        out_specs=[hbm, hbm, vmem],
        out_shape=[
            shape(f32, rows, D),
            shape(f32, rows, D),
            shape(f32, ADAPTERS // fsdp, padded, 128),
        ],
        scratch_shapes=[
            pltpu.VMEM((rows, 128), f32),
            pltpu.VMEM((rows, 128), f32),
            pltpu.VMEM((tree, width), bf),
            pltpu.VMEM((tree, width), bf),
            pltpu.VMEM((D, 3 * width), bf),
            pltpu.VMEM((D, width), bf),
            pltpu.VMEM((max(fsdp, contexts) * half, D), bf),
            pltpu.VMEM((max(fsdp, contexts) * half, D), bf),
            pltpu.VMEM((max(fsdp - 1, 2) * half, D), bf),
            pltpu.VMEM((fsdp * half, D), bf),
            pltpu.VMEM((fsdp * half, D), bf),
            pltpu.VMEM(((fsdp - 1) * half, D), bf),
            pltpu.VMEM((half, D), bf),
            pltpu.VMEM((rows, D), bf),
            pltpu.VMEM((half, D), bf),
            pltpu.VMEM((rows, D), bf),
            pltpu.VMEM((rows, D), f32),
            pltpu.VMEM((rows, width), bf),
            pltpu.VMEM((width, rows), bf),
            pltpu.VMEM((8, rows), f32),
            pltpu.VMEM((8, rows), f32),
            pltpu.VMEM((width, rows), bf),
            pltpu.VMEM((width, rows), f32),
            pltpu.VMEM((contexts * half, D), bf),
            pltpu.VMEM((contexts * half, D), bf),
            pltpu.VMEM((rows, D), bf),
            dma((2, moves)),
            dma((2, moves)),
            dma((contexts,)),
            dma((contexts,)),
            dma((3, slots)),
            dma((3, slots)),
            dma((contexts,)),
            dma((contexts,)),
            dma((3, slots)),
            dma((5, contexts)),
            pltpu.VMEM((rows, D), bf),
            pltpu.VMEM((rows, D), bf),
            pltpu.VMEM((rows, D), f32),
            pltpu.VMEM((rows, D), bf),
            pltpu.VMEM((rows, D), bf),
            pltpu.VMEM((width, rows), bf),
            pltpu.VMEM((rows, width), bf),
            pltpu.VMEM((rows, width), bf),
            pltpu.VMEM((width, rows), f32),
            pltpu.VMEM((D, 128), bf),
            pltpu.VMEM((256, 3 * width), bf),
            pltpu.VMEM((256, D), bf),
            pltpu.VMEM((width, 128), bf),
            pltpu.VMEM((256, width), bf),
            pltpu.VMEM((256, D), bf),
            pltpu.VMEM((3 * RANK, D), f32),
            pltpu.VMEM((3 * RANK, width), f32),
            pltpu.VMEM((RANK, width), f32),
            pltpu.VMEM((RANK, D), f32),
            pltpu.VMEM((PARAMS // 128, 128), f32),
            pltpu.VMEM((max(D, units), 128), f32),
            pltpu.VMEM((contexts, 2, padded, 128), f32),
            pltpu.VMEM((contexts, padded, 128), f32),
            pltpu.VMEM((contexts - 1, padded, 128), bf),
            pltpu.VMEM((contexts - 1, padded, 128), bf),
            pltpu.VMEM((padded, 128), bf),
            pltpu.VMEM((fsdp - 1, padded, 128), bf),
            dma((17,)),
            dma((3, max(fsdp, contexts))),
            dma((3, max(fsdp, contexts))),
            pltpu.VMEM((width // HEAD_DIM, rows, rows), bf),
            dma((width // HEAD_DIM // 2,)),
            pltpu.VMEM((rows, D), bf),
            pltpu.VMEM((rows, D), bf),
        ],
        name="backward",
        compiler_params=pltpu.CompilerParams(
            collective_id=3, has_side_effects=True, vmem_limit_bytes=63 << 20
        ),
    )(*remote, *local)


def shards(
    tokens,
    attn_gain,
    w_qkv,
    w_out,
    ffn_gain,
    w_gu,
    w_dn,
    w_egu,
    w_edn,
    adapters,
    adapter_ids,
    parents,
    seg_lengths,
    routes,
    route_weights,
    cotangent,
):
    row_count = tokens.shape[1]
    contexts = lax.axis_size("context")
    tensors = lax.axis_size("tensor")
    fsdp_size = lax.axis_size("fsdp")
    sizes = (fsdp_size, contexts, tensors)
    local_width = w_qkv.shape[2]
    local_ff = w_dn.shape[0]
    own_adapters = adapters.shape[0]
    own_width = D // fsdp_size
    gains = jnp.broadcast_to(jnp.concatenate([attn_gain, ffn_gain])[None], (16, 2 * own_width))
    route_table = jnp.concatenate(
        [
            routes[0].astype(jnp.float32).T,
            route_weights[0].astype(jnp.float32).T,
            jnp.broadcast_to(adapter_ids.astype(jnp.float32)[:, None], (1, row_count)),
            jnp.zeros((3, row_count), jnp.float32),
        ]
    )
    lines = adapters.shape[1] // 128
    padded = (lines + 15) // 16 * 16
    adapter_rows = jnp.pad(
        adapters.reshape(own_adapters, lines, 128), ((0, 0), (0, padded - lines), (0, 0))
    ).reshape(own_adapters * padded, 128)
    half_dim = HEAD_DIM // 2
    frequency = rope_base ** (-(jnp.arange(half_dim, dtype=jnp.float32) * 2.0) / HEAD_DIM)
    signs = jnp.concatenate([-jnp.ones((half_dim,)), jnp.ones((half_dim,))])
    turns = jnp.concatenate(
        [jnp.tile(frequency, 4)[None], jnp.tile(signs, 2)[None], jnp.zeros((6, 128))]
    ).astype(jnp.float32)
    sharded = (
        tokens[0],
        cotangent[0],
        w_qkv.reshape(own_width, 3 * local_width),
        w_out.T,
        w_gu.reshape(own_width, 2 * local_ff),
        w_dn.T,
    )
    (
        n1_all,
        k_all,
        v_all,
        wq_all,
        wo_all,
        normed_all,
        cotangent_all,
        p_all,
        q_t,
        q_n,
        mixed_own,
        o_t,
        lse,
        resid,
        shared,
        dn2,
        da_gu_t,
        db_gu_own,
        da_dn_t,
        db_dn_own,
        gains_full,
        cosine,
        sinus,
        hot,
        reach_t,
        a_qkv,
        b_qkv2,
        a_qkv_t2,
        a_o,
        b_o2,
        a_o_t2,
        table_all,
        place_row,
        place_col,
        weight_col,
        marks,
        peaks,
    ) = forward_call(
        sizes,
        sharded,
        (adapter_rows, gains, route_table, turns, adapter_ids, parents, seg_lengths),
    )
    own_experts = EXPERTS // fsdp_size
    starts = marks[:own_experts].astype(jnp.int32)
    moe_all, moe_back_all = moe_call(
        starts,
        place_row,
        place_col,
        weight_col,
        normed_all,
        cotangent_all,
        w_egu.transpose(0, 2, 1, 3),
        w_edn,
    )
    remote = (moe_all, moe_back_all, n1_all, k_all, v_all, wq_all, wo_all, cosine, sinus, p_all)
    block_out, input_grad, sums = backward_call(
        sizes,
        remote,
        (tokens[0], cotangent[0], gains_full, peaks)
        + (resid, shared, dn2, q_t, q_n, mixed_own, o_t, lse)
        + (a_qkv, b_qkv2, a_qkv_t2, a_o, a_o_t2, b_o2)
        + (da_gu_t, db_gu_own, da_dn_t, db_dn_own, table_all),
    )
    adapter_grads = sums[:, :lines].reshape(own_adapters, -1)
    return (block_out[None], input_grad[None], adapter_grads)


def solution(mesh):
    return jax.shard_map(
        shards,
        mesh=mesh,
        in_specs=(
            P("fsdp", "context", None),
            P("fsdp"),
            P("fsdp", None, "tensor"),
            P("tensor", "fsdp"),
            P("fsdp"),
            P("fsdp", None, "tensor"),
            P("tensor", "fsdp"),
            P("fsdp", None, None, "tensor"),
            P("fsdp", "tensor", None),
            P("fsdp", ("context", "tensor")),
            P("fsdp"),
            P("fsdp", None),
            P("fsdp", None),
            P("fsdp", "context", None),
            P("fsdp", "context", None),
            P("fsdp", "context", None),
        ),
        out_specs=(
            P("fsdp", "context", None),
            P("fsdp", "context", None),
            P("fsdp", ("context", "tensor")),
        ),
        check_vma=False,
    )
```

profile of v0, /device:TPU:0, one launch (start us, length us, event | category | flops | bytes accessed | tf_op | source)
XLA Modules:
  0.0 263.3 jit_solution(16436634132869594912)
XLA Ops:
  1.4 0.1 pad.7.clone
  1.5 0.1 pad.11.clone
  1.6 0.8 pad_maximum_fusion
  2.4 0.7 tile.5
  3.0 0.1 broadcast_in_dim_tile.7
  3.1 0.1 broadcast_in_dim_tile.6
  3.2 0.7 maximum_maximum_fusion.1.turns
  3.8 0.7 convert_bitcast_fusion.1
  4.5 0.7 convert_bitcast_fusion
  5.2 0.7 maximum_maximum_fusion.table_in
  5.9 0.6 broadcast_in_dim.26.gains_in
  6.5 1.0 reshape.37
  7.5 0.7 pad.4
  8.1 1.8 copy.23
  10.0 1.1 copy.24
  11.0 7.5 %copy.28 = bf16[2,768,2,1024]{3,1,2,0:T(8,128)(2,1)} copy(bf16[2,768,2,1024]{3,2,1,0:T(2,128)(2,1)} %param.23) | data formatting | bytes 12582912 | tf_op args[7]
  18.5 96.5 %forward.1 = (bf16[2560,768]{1,0:T(8,128)(2,1)}, bf16[2560,384]{1,0:T(8,128)(2,1)}, bf16[2560,384]{1,0:T(8,128)(2,1)}, bf16[768,1152]{1,0:T(8,128)(2,1)}, bf16[7...) custom-call(bf16[640,768]{1,0:T(8,128)(2,1)} %bitcast.30, ...), custom_call_target="tpu_custom_call" | custom-call | tf_op jit(solution)/shard_map/forward/pallas_call | solution.py:1250
  115.0 1.2 slice_convert_fusion.starts
  116.3 36.6 %experts.1 = (bf16[2560,768]{1,0:T(8,128)(2,1)}, bf16[2560,768]{1,0:T(8,128)(2,1)}) custom-call(s32[2,128]{1,0:T(2,128)} %slice_convert_fusion.starts, f32[8,2560]{1,0:T(8,128)} %get-tuple-element.44.place_row, f32[2560,128]{1,0:T(8,128)} %get-tuple-element.45.place_hbm, bf16[2560,128]{1,0:T(8,128)(2,1)} %get-tuple-element.46.weight_hbm, ...), custom_call_target="tpu_custom_call" | custom-call | tf_op jit(solution)/shard_map/experts/pallas_call | solution.py:266
  152.9 104.0 %backward.1 = (f32[640,768]{1,0:T(8,128)}, f32[640,768]{1,0:T(8,128)}, f32[2,240,128]{2,1,0:T(8,128)}) custom-call(bf16[2560,768]{1,0:T(8,128)(2,1)} %get-tuple-element.49.moe_out, bf16[2560,768]{1,0:T(8,128)(2,1)} %get-tuple-element.50.moe_back, bf16[2560,768]{1,0:T(8,128)(2,1)} %get-tuple-element.51.n1_hbm, bf16[2560,384]{1,0:T(8,128)(2,1)} %get-tuple-element.52.k_hbm, ...), custom_call_target="tpu_custom_call" | custom-call | tf_op jit(solution)/shard_map/backward/pallas_call | solution.py:2156
  256.9 1.0 slice_bitcast_fusion
  257.9 0.8 copy.29
  258.7 3.1 %copy.33 = f32[1,640,768]{2,1,0:T(8,128)} copy(f32[1,640,768]{2,1,0:T(8,128)} %bitcast.36) | data formatting | bytes 3932160
  261.8 1.3 copy.34
  (9 shorter events, 0.1 us)
Async XLA Ops:
  0.6 9.3 %copy-start.1 = (bf16[192,2,1024]{2,1,0:T(2,128)(2,1)S(1)}, bf16[192,2,1024]{2,1,0:T(2,128)(2,1)}, u32[]{:S(2)}) copy-start(bf16[192,2,1024]{2,1,0:T(2,128)(2,1)} %param.21) | copy-start | bytes 2359300
  258.7 3.1 %copy-start = (f32[640,768]{1,0:T(8,128)S(1)}, f32[640,768]{1,0:T(8,128)}, u32[]{:S(2)}) copy-start(f32[640,768]{1,0:T(8,128)} %get-tuple-element.81) | copy-start | bytes 5898244
where the time goes:
time: 268 us; the launch traced here: 263 us
  Pallas kernels  237 us (88%)
  local copies, waits for them, and re-layouts  19.8 us (7%)
  other arithmetic  4.71 us (2%)
    pallas_call x1, Pallas kernels, backward_call(): pl.pallas_call(functools.partial(backward_kernel, sizes), in_specs=[hbm]...  104 us
    pallas_call x1, Pallas kernels, forward_call(): pl.pallas_call(functools.partial(forward_kernel, sizes), in_specs=[hbm] *...  96.5 us
    pallas_call x1, Pallas kernels, moe_call(): pl.pallas_call(moe_kernel, grid_spec=pltpu.PrefetchScalarGridSpec(num_sca...  36.6 us
    unnamed x10, local copies, waits for them, and re-layouts  14.7 us

commit v1 on v0

--- a/solution.py
+++ b/solution.py
@@ -1,5 +1,6 @@
 import jax
 import jax.numpy as jnp
+import numpy as np
 import functools
 import math
 
@@ -456,14 +457,13 @@
     reach_t[...] = nt_dot(ancestors, hot[own, :]).astype(jnp.bfloat16)
 
 
-def choose(ids, adapters_all, out):
-    wanted = ids[0]
-    own = ADAPTERS // adapters_all.shape[0]
-    count = adapters_all.shape[1] // own
+def choose(f, wanted, adapters, out):
+    count = out.shape[0]
+    own = adapters.shape[0] // count
     total = jnp.zeros((count, 128), jnp.float32)
-    for a in range(ADAPTERS):
-        block = adapters_all[a // own, pl.ds((a % own) * count, count), :].astype(jnp.float32)
-        total = total + jnp.where(wanted == a, block, 0.0)
+    for a in range(own):
+        block = adapters[a * count : (a + 1) * count, :].astype(jnp.float32)
+        total = total + jnp.where(wanted == (f * own + a).astype(jnp.float32), block, 0.0)
     out[...] = total.astype(jnp.bfloat16)
 
 
@@ -497,7 +497,7 @@
                 at = token % rows
                 found = jnp.where(lane == token // TOKEN_TILE + 1, count[:, at : at + 1], found)
         base = count[:, rows - 1 : rows]
-    marks[...] = found
+    marks[...] = found.astype(jnp.int32)
 
 
 def unpack_adapter(t, per_block, chosen, flat, wide, first, second):
@@ -580,7 +580,6 @@
     gains_in,
     table_in,
     turns,
-    ids,
     parents,
     lengths,
     n1_all,
@@ -639,6 +638,7 @@
     shared,
     dn2,
     adapters_all,
+    picked,
     gains_all,
     chosen,
     flat,
@@ -800,11 +800,9 @@
         bits, f, peer, n2_own, n2_all, rows, t * half, half, fs_send.at[5], fs_recv.at[5]
     )
     wq_gather, wo_gather, gu_gather, dn_gather = gathers
-    small = []
+    small, rows_sent = [], []
     for k, other in enumerate(peers):
-        for j, (source, target) in enumerate(
-            ((adapters_in, adapters_all), (gains_in, gains_all), (table_in, table_all))
-        ):
+        for j, (source, target) in enumerate(((table_in, table_all), (gains_in, gains_all))):
             copy = send(source, target.at[f], small_send.at[j, k], small_recv.at[j, k], other)
             copy.start()
             small.append(copy)
@@ -828,9 +826,18 @@
     db_gu[...] = jnp.zeros_like(db_gu)
     da_dn[...] = jnp.zeros_like(da_dn)
     db_dn[...] = jnp.zeros_like(db_dn)
-    adapters_all[f] = adapters_in[...]
     gains_all[f] = gains_in[...]
     table_all[f] = table_in[...]
+    for copy in small:
+        copy.wait_recv()
+    for k, other in enumerate(peers):
+        choose(f, table_all[lax.rem(f + k + 1, fsdp), 4:5, 0:1], adapters_in, picked.at[k])
+        copy = send(
+            picked.at[k], adapters_all.at[f], small_send.at[2, k], small_recv.at[2, k], other
+        )
+        copy.start()
+        rows_sent.append(copy)
+    choose(f, table_all[f, 4:5, 0:1], adapters_in, adapters_all.at[f])
     tree_tables(parents, lengths, turns, c, rows, hot, reach_t, cosine, sinus)
 
     def receive(step):
@@ -931,9 +938,12 @@
                 gather.wait(stage)
         following.start(0)
 
-    for copy in small:
+    for copy in rows_sent:
         copy.wait_recv()
-    choose(ids, adapters_all, chosen.at[t, c])
+    total_row = adapters_all[0].astype(jnp.float32)
+    for b in range(1, fsdp):
+        total_row = total_row + adapters_all[b].astype(jnp.float32)
+    chosen[t, c] = total_row.astype(jnp.bfloat16)
     spread = []
     for k, other in enumerate(stacked):
         block = chosen.at[t, c]
@@ -1178,7 +1188,7 @@
     pass_pieces(n2_gather, n2_forward, bits - 1)
     for copy in n2_forward + g_forward:
         copy.wait()
-    for copy in small + spread + [shared_copy]:
+    for copy in small + rows_sent + spread + [shared_copy]:
         copy.wait_send()
     for group in gu_lent:
         for copy in group:
@@ -1249,7 +1259,7 @@
     hops = contexts + 5 + 2 * moves
     return pl.pallas_call(
         functools.partial(forward_kernel, sizes),
-        in_specs=[hbm] * 6 + [vmem] * 4 + [smem] * 3,
+        in_specs=[hbm] * 6 + [vmem] * 4 + [smem] * 2,
         out_specs=[hbm] * 8 + [hbm, hbm, hbm, hbm, hbm, hbm, hbm, hbm, vmem, vmem, vmem, vmem, hbm, hbm, hbm, hbm, hbm, hbm, hbm, hbm, hbm, hbm, hbm, hbm, hbm, hbm, hbm, vmem, vmem],
         out_shape=[
             shape(bf, tree, D),
@@ -1287,7 +1297,7 @@
             shape(f32, 8, total),
             shape(f32, total, 128),
             shape(bf, total, 128),
-            shape(f32, 8, 128),
+            shape(jnp.int32, 8, 128),
             shape(f32, contexts * 8, rows),
         ],
         scratch_shapes=[
@@ -1309,7 +1319,8 @@
             pltpu.VMEM((rows, D), bf),
             pltpu.VMEM((rows, D), bf),
             pltpu.VMEM((rows, D), bf),
-            pltpu.VMEM((fsdp,) + adapters.shape, bf),
+            pltpu.VMEM((fsdp, per_adapter, 128), bf),
+            pltpu.VMEM((fsdp - 1, per_adapter, 128), bf),
             pltpu.VMEM((fsdp,) + gains.shape, bf),
             pltpu.VMEM((2, contexts, per_adapter, 128), bf),
             pltpu.VMEM((PARAMS // 128, 128), f32),
@@ -1553,6 +1564,7 @@
     factor,
     k_t,
     dq_t,
+    dq,
     part_in,
     z_in,
     dn1_full,
@@ -1942,10 +1954,9 @@
 
         lax.fori_loop(0, heads // 2, pair_step, 0)
 
-    def project_back(chunk, own):
+    def adapter_back(chunk, own):
         block = chunk_rows(chunk)
         grads = grad_kv[kv_rows, :]
-        result = nt_dot(grads, wq[:, width:])
         rank_back = nt_dot(grads, b_qkv2[0:128, width:])
         n1_load(chunk).wait()
         n1 = n1_buf[...]
@@ -1954,19 +1965,20 @@
         db_qkv[RANK : 2 * RANK, :] += both[RANK : 2 * RANK, :width]
         db_qkv[2 * RANK :, :] += both[2 * RANK : 3 * RANK, width:]
         if own:
-            pieces = []
             for p in range(width // 128):
                 lanes = slice(128 * p, 128 * p + 128)
                 grad_query = (dq_t[lanes, :] * 0.125).T
-                pieces.append(
-                    turn(grad_query, cosine[...], -sinus[...]).astype(bf)
-                )
-            grad_query = jnp.concatenate(pieces, axis=1)
-            result += nt_dot(grad_query, wq[:, :width])
-            rank_back += nt_dot(grad_query, b_qkv2[0:128, :width])
-            db_qkv[0:RANK, :] += 2.0 * tn_dot(rank, grad_query)[0:RANK, :]
+                dq[:, lanes] = turn(grad_query, cosine[...], -sinus[...]).astype(bf)
+            rank_back += nt_dot(dq[...], b_qkv2[0:128, :width])
+            db_qkv[0:RANK, :] += 2.0 * tn_dot(rank, dq[...])[0:RANK, :]
+        da_qkv[...] += tn_dot(rank_back.astype(bf), n1)[0 : 3 * RANK]
+        return rank_back
+
+    def project_back(chunk, own, rank_back):
+        result = nt_dot(grad_kv[kv_rows, :], wq[:, width:])
+        if own:
+            result += nt_dot(dq[...], wq[:, :width])
         result += nn_dot(two_parts(rank_back), a_qkv_t2[...])
-        da_qkv[...] += tn_dot(rank_back.astype(bf), n1)[0 : 3 * RANK]
         part[...] = result.astype(bf)
         part_out[work_rows(chunk), :] = part[theirs, :]
         z_out[work_rows(chunk), :] = part[mine, :]
@@ -1980,26 +1992,36 @@
             sibling,
         )
 
-    def down(chunk):
-        block = work_rows(chunk)
+    pieces = split_rows(half)
+
+    def down(chunk, piece):
+        offset, size = pieces[piece]
+        block = Gather.rows(chunk * half + offset, size)
         return send(
-            z_out.at[block], z_in.at[block], z_send.at[chunk], z_recv.at[chunk], (f, c - 1, t)
+            z_out.at[block],
+            z_in.at[block],
+            z_send.at[chunk, piece],
+            z_recv.at[chunk, piece],
+            (f, c - 1, t),
         )
 
-    def chain(chunk):
-        block = work_rows(chunk)
+    def chain(chunk, onward):
         pair_copy(chunk).wait_recv()
-        summed = z_out[block, :].astype(f32) + part_in[block, :].astype(f32)
-        z_out[block, :] = summed.astype(bf)
-
-        @pl.when(c < contexts - 1)
-        def _():
-            down(chunk).wait_recv()
-            z_out[block, :] = (summed + z_in[block, :].astype(f32)).astype(bf)
+        for piece, (offset, size) in enumerate(pieces):
+            block = Gather.rows(chunk * half + offset, size)
+            summed = z_out[block, :].astype(f32) + part_in[block, :].astype(f32)
+            z_out[block, :] = summed.astype(bf)
+
+            @pl.when(c < contexts - 1)
+            def _(block=block, summed=summed, piece=piece):
+                down(chunk, piece).wait_recv()
+                z_out[block, :] = (summed + z_in[block, :].astype(f32)).astype(bf)
+
+            if onward:
+                down(chunk, piece).start()
 
     def pass_down(chunk):
-        chain(chunk)
-        down(chunk).start()
+        chain(chunk, True)
 
     def sum_moe():
         for stage in range(1, bits):
@@ -2015,7 +2037,7 @@
 
     def step(chunk, carry):
         attend_back(chunk)
-        project_back(chunk, False)
+        project_back(chunk, False, adapter_back(chunk, False))
         pair_copy(chunk).start()
 
         @pl.when(c == contexts - 1)
@@ -2042,12 +2064,16 @@
 
     lax.fori_loop(0, c, step, 0)
     attend_back(c)
-    project_back(c, True)
-    pair_copy(c).start()
+    last_rank = adapter_back(c, True)
     pack_first(t, flat, wide, da_qkv, db_qkv, da_o, db_o)
     fill_blocks(0, early)
     for block in range(early):
         pair_block(block).start()
+    project_back(c, True, last_rank)
+    pair_copy(c).start()
+    for block in range(early):
+        pair_block(block).wait_recv()
+    push_blocks(False)
 
     @pl.when((c < 2) & (c >= early))
     def _():
@@ -2061,15 +2087,11 @@
     def _():
         pass_down(c - 1)
 
-    for block in range(early):
-        pair_block(block).wait_recv()
-    push_blocks(False)
-
     @pl.when(c < 2)
     def _():
         share_moe()
 
-    chain(c)
+    chain(c, False)
     dn1_full[mine, :] = z_out[work_rows(c), :]
     dn1_copy = send(
         z_out.at[work_rows(c)],
@@ -2128,7 +2150,8 @@
 
         @pl.when(chunk < c)
         def _():
-            down(chunk).wait_send()
+            for piece in range(len(pieces)):
+                down(chunk, piece).wait_send()
 
         return carry
 
@@ -2186,13 +2209,14 @@
             pltpu.VMEM((8, rows), f32),
             pltpu.VMEM((width, rows), bf),
             pltpu.VMEM((width, rows), f32),
+            pltpu.VMEM((rows, width), bf),
             pltpu.VMEM((contexts * half, D), bf),
             pltpu.VMEM((contexts * half, D), bf),
             pltpu.VMEM((rows, D), bf),
             dma((2, moves)),
             dma((2, moves)),
-            dma((contexts,)),
-            dma((contexts,)),
+            dma((contexts, 2)),
+            dma((contexts, 2)),
             dma((3, slots)),
             dma((3, slots)),
             dma((contexts,)),
@@ -2283,11 +2307,11 @@
         adapters.reshape(own_adapters, lines, 128), ((0, 0), (0, padded - lines), (0, 0))
     ).reshape(own_adapters * padded, 128)
     half_dim = HEAD_DIM // 2
-    frequency = rope_base ** (-(jnp.arange(half_dim, dtype=jnp.float32) * 2.0) / HEAD_DIM)
-    signs = jnp.concatenate([-jnp.ones((half_dim,)), jnp.ones((half_dim,))])
-    turns = jnp.concatenate(
-        [jnp.tile(frequency, 4)[None], jnp.tile(signs, 2)[None], jnp.zeros((6, 128))]
-    ).astype(jnp.float32)
+    exponents = -(np.arange(half_dim, dtype=np.float32) * np.float32(2.0)) / np.float32(HEAD_DIM)
+    frequency = np.power(np.float32(rope_base), exponents).astype(np.float32)
+    signs = np.repeat(np.array([-1.0, 1.0], np.float32), half_dim)
+    turns = np.zeros((8, 128), np.float32)
+    turns[0], turns[1] = np.tile(frequency, 4), np.tile(signs, 2)
     sharded = (
         tokens[0],
         cotangent[0],
@@ -2337,12 +2361,10 @@
     ) = forward_call(
         sizes,
         sharded,
-        (adapter_rows, gains, route_table, turns, adapter_ids, parents, seg_lengths),
+        (adapter_rows, gains, route_table, turns, parents, seg_lengths),
     )
-    own_experts = EXPERTS // fsdp_size
-    starts = marks[:own_experts].astype(jnp.int32)
     moe_all, moe_back_all = moe_call(
-        starts,
+        marks,
         place_row,
         place_col,
         weight_col,

time: 268 us -> 266 us (level)
  Pallas kernels: 237 us -> 241 us
    pallas_call x1, Pallas kernels: 104 us -> 114 us  [backward_call(): pl.pallas_call(functools.partial(backward_kernel, sizes), in_specs=[hbm]...]
    pallas_call x1, Pallas kernels: 36.6 us -> 31.7 us  [moe_call(): pl.pallas_call(moe_kernel, grid_spec=pltpu.PrefetchScalarGridSpec(num_sca...]
where the time goes in v1:
time: 266 us; the launch traced here: 264 us
  Pallas kernels  241 us (91%)
  local copies, waits for them, and re-layouts  18.9 us (7%)
  other arithmetic  2.8 us (1%)
    pallas_call x1, Pallas kernels, backward_call(): pl.pallas_call(functools.partial(backward_kernel, sizes), in_specs=[hbm]...  114 us
    pallas_call x1, Pallas kernels, forward_call(): pl.pallas_call(functools.partial(forward_kernel, sizes), in_specs=[hbm] *...  95.1 us
    pallas_call x1, Pallas kernels, moe_call(): pl.pallas_call(moe_kernel, grid_spec=pltpu.PrefetchScalarGridSpec(num_sca...  31.7 us
    unnamed x10, local copies, waits for them, and re-layouts  14.7 us

profile of v1, /device:TPU:0, one launch (start us, length us, event | category | flops | bytes accessed | tf_op | source)
XLA Modules:
  0.0 263.8 jit_solution(15635308316404109762)
XLA Ops:
  0.6 0.0 copy-start.1
  1.4 0.1 pad.7.clone
  1.4 0.1 pad.8.clone
  1.5 0.7 pad_maximum_fusion
  2.3 0.7 convert_bitcast_fusion.1
  3.0 0.7 convert_bitcast_fusion
  3.6 0.7 maximum_maximum_fusion.table_in
  4.3 0.6 broadcast_in_dim.23.gains_in
  4.9 1.0 reshape.30
  5.9 0.7 pad.4
  6.6 1.8 copy.24
  8.4 0.0 copy-done.1
  8.4 1.1 copy.25
  9.5 7.5 %copy.29 = bf16[2,768,2,1024]{3,1,2,0:T(8,128)(2,1)} copy(bf16[2,768,2,1024]{3,2,1,0:T(2,128)(2,1)} %param.24) | data formatting | bytes 12582912 | tf_op args[7]
  16.9 95.1 %forward.1 = (bf16[2560,768]{1,0:T(8,128)(2,1)}, bf16[2560,384]{1,0:T(8,128)(2,1)}, bf16[2560,384]{1,0:T(8,128)(2,1)}, bf16[768,1152]{1,0:T(8,128)(2,1)}, bf16[7...) custom-call(bf16[640,768]{1,0:T(8,128)(2,1)} %bitcast.30, ...), custom_call_target="tpu_custom_call" | custom-call | tf_op jit(solution)/shard_map/forward/pallas_call | solution.py:1260
  112.0 31.7 %experts.1 = (bf16[2560,768]{1,0:T(8,128)(2,1)}, bf16[2560,768]{1,0:T(8,128)(2,1)}) custom-call(s32[8,128]{1,0:T(8,128)} %get-tuple-element.43.starts, f32[8,2560]{1,0:T(8,128)} %get-tuple-element.44.place_row, f32[2560,128]{1,0:T(8,128)} %get-tuple-element.45.place_hbm, bf16[2560,128]{1,0:T(8,128)(2,1)} %get-tuple-element.46.weight_hbm, ...), custom_call_target="tpu_custom_call" | custom-call | tf_op jit(solution)/shard_map/experts/pallas_call | solution.py:267
  143.7 113.7 %backward.1 = (f32[640,768]{1,0:T(8,128)}, f32[640,768]{1,0:T(8,128)}, f32[2,240,128]{2,1,0:T(8,128)}) custom-call(bf16[2560,768]{1,0:T(8,128)(2,1)} %get-tuple-element.49.moe_out, bf16[2560,768]{1,0:T(8,128)(2,1)} %get-tuple-element.50.moe_back, bf16[2560,768]{1,0:T(8,128)(2,1)} %get-tuple-element.51.n1_hbm, bf16[2560,384]{1,0:T(8,128)(2,1)} %get-tuple-element.52.k_hbm, ...), custom_call_target="tpu_custom_call" | custom-call | tf_op jit(solution)/shard_map/backward/pallas_call | solution.py:2179
  257.4 1.0 slice_bitcast_fusion
  258.4 0.8 copy.30
  259.2 0.0 copy-start
  259.2 3.1 %copy.34 = f32[1,640,768]{2,1,0:T(8,128)} copy(f32[1,640,768]{2,1,0:T(8,128)} %bitcast.36) | data formatting | bytes 3932160
  262.3 0.0 copy-done
  262.3 1.3 copy.35
  (1 shorter events, 0.0 us)
Async XLA Ops:
  0.6 7.7 %copy-start.1 = (bf16[192,2,1024]{2,1,0:T(2,128)(2,1)S(1)}, bf16[192,2,1024]{2,1,0:T(2,128)(2,1)}, u32[]{:S(2)}) copy-start(bf16[192,2,1024]{2,1,0:T(2,128)(2,1)} %param.22) | copy-start | bytes 2359300
  259.2 3.1 %copy-start = (f32[640,768]{1,0:T(8,128)S(1)}, f32[640,768]{1,0:T(8,128)}, u32[]{:S(2)}) copy-start(f32[640,768]{1,0:T(8,128)} %get-tuple-element.81) | copy-start | bytes 5898244

commit v2 on v1

--- a/solution.py
+++ b/solution.py
@@ -1538,7 +1538,7 @@
     da_dn,
     db_dn,
     table_all,
-    block_out,
+    ffn_out,
     input_grad,
     adapter_out,
     cosine,
@@ -1954,10 +1954,11 @@
 
         lax.fori_loop(0, heads // 2, pair_step, 0)
 
-    def adapter_back(chunk, own):
-        block = chunk_rows(chunk)
+    def ranks():
+        return nt_dot(grad_kv[kv_rows, :], b_qkv2[0:128, width:])
+
+    def adapter_back(chunk, own, rank_back):
         grads = grad_kv[kv_rows, :]
-        rank_back = nt_dot(grads, b_qkv2[0:128, width:])
         n1_load(chunk).wait()
         n1 = n1_buf[...]
         rank = nn_dot(n1, a_qkv[...]).astype(bf)
@@ -2037,8 +2038,10 @@
 
     def step(chunk, carry):
         attend_back(chunk)
-        project_back(chunk, False, adapter_back(chunk, False))
+        rank_back = ranks()
+        project_back(chunk, False, rank_back)
         pair_copy(chunk).start()
+        adapter_back(chunk, False, rank_back)
 
         @pl.when(c == contexts - 1)
         def _():
@@ -2064,7 +2067,7 @@
 
     lax.fori_loop(0, c, step, 0)
     attend_back(c)
-    last_rank = adapter_back(c, True)
+    last_rank = adapter_back(c, True, ranks())
     pack_first(t, flat, wide, da_qkv, db_qkv, da_o, db_o)
     fill_blocks(0, early)
     for block in range(early):
@@ -2102,9 +2105,13 @@
     )
     dn1_copy.start()
     ffn_copy.wait_recv()
-    resid[...] = resid[...] + ffn_full[...].astype(f32)
-    block_copy = pltpu.make_async_copy(resid, block_out, in_sems.at[len(inputs)])
+    block_copy = pltpu.make_async_copy(ffn_full, ffn_out, in_sems.at[len(inputs)])
     block_copy.start()
+
+    @pl.when(c < early)
+    def _():
+        sum_own()
+
     dn1_copy.wait_recv()
 
     def final_tile(i, carry):
@@ -2118,10 +2125,6 @@
     lax.fori_loop(0, 2, final_tile, 0)
     grad_copy = pltpu.make_async_copy(dy, input_grad, in_sems.at[len(inputs) + 1])
     grad_copy.start()
-    @pl.when(c < early)
-    def _():
-        sum_own()
-
     own = ADAPTERS // fsdp
     wanted = [(f * own + a).astype(f32) for a in range(own)]
     mine_sum = own_sum[...].astype(f32)
@@ -2181,7 +2184,7 @@
         in_specs=[hbm] * len(remote) + [hbm, hbm, vmem, vmem, hbm, hbm, hbm, hbm, hbm, hbm, hbm, vmem, hbm, hbm, hbm, hbm, hbm, hbm, vmem, vmem, vmem, vmem, vmem],
         out_specs=[hbm, hbm, vmem],
         out_shape=[
-            shape(f32, rows, D),
+            shape(bf, rows, D),
             shape(f32, rows, D),
             shape(f32, ADAPTERS // fsdp, padded, 128),
         ],
@@ -2374,7 +2377,7 @@
         w_edn,
     )
     remote = (moe_all, moe_back_all, n1_all, k_all, v_all, wq_all, wo_all, cosine, sinus, p_all)
-    block_out, input_grad, sums = backward_call(
+    ffn_sum, input_grad, sums = backward_call(
         sizes,
         remote,
         (tokens[0], cotangent[0], gains_full, peaks)
@@ -2383,6 +2386,7 @@
         + (da_gu_t, db_gu_own, da_dn_t, db_dn_own, table_all),
     )
     adapter_grads = sums[:, :lines].reshape(own_adapters, -1)
+    block_out = resid + ffn_sum.astype(jnp.float32)
     return (block_out[None], input_grad[None], adapter_grads)
 
 

time: 266 us -> 266 us (level)
  local copies, waits for them, and re-layouts: 18.9 us -> 14.9 us
  other arithmetic: 2.8 us -> 6.2 us
    pallas_call x1, Pallas kernels: 114 us -> 118 us  [backward_call(): pl.pallas_call(functools.partial(backward_kernel, sizes), in_specs=[hbm]...]
    unnamed x10 -> x11, local copies, waits for them, and re-layouts: 14.7 us -> 10.7 us
    broadcast_in_dim x0 -> x1, other arithmetic: none -> 3.4 us  [shards(): return (block_out[None], input_grad[None], adapter_grads)]
    pallas_call x1, Pallas kernels: 31.7 us -> 28.6 us  [moe_call(): pl.pallas_call(moe_kernel, grid_spec=pltpu.PrefetchScalarGridSpec(num_sca...]
where the time goes in v2:
time: 266 us; the launch traced here: 264 us
  Pallas kernels  242 us (91%)
  local copies, waits for them, and re-layouts  14.9 us (6%)
  other arithmetic  6.2 us (2%)
    pallas_call x1, Pallas kernels, backward_call(): pl.pallas_call(functools.partial(backward_kernel, sizes), in_specs=[hbm]...  118 us
    pallas_call x1, Pallas kernels, forward_call(): pl.pallas_call(functools.partial(forward_kernel, sizes), in_specs=[hbm] *...  95.1 us
    pallas_call x1, Pallas kernels, moe_call(): pl.pallas_call(moe_kernel, grid_spec=pltpu.PrefetchScalarGridSpec(num_sca...  28.6 us
    unnamed x11, local copies, waits for them, and re-layouts  10.7 us

profile of v2, /device:TPU:0, one launch (start us, length us, event | category | flops | bytes accessed | tf_op | source)
XLA Modules:
  0.0 264.3 jit_solution(649133456866471081)
XLA Ops:
  0.6 0.0 copy-start.1
  1.4 0.1 pad.7.clone
  1.4 0.1 pad.8.clone
  1.5 0.7 pad_maximum_fusion
  2.3 0.7 convert_bitcast_fusion.1
  3.0 0.7 convert_bitcast_fusion
  3.6 0.7 maximum_maximum_fusion.table_in
  4.3 0.6 broadcast_in_dim.23.gains_in
  4.9 1.0 reshape.30
  5.9 0.7 pad.4
  6.6 1.8 copy.24
  8.4 0.0 copy-done.1
  8.4 1.1 copy.25
  9.5 7.5 %copy.29 = bf16[2,768,2,1024]{3,1,2,0:T(8,128)(2,1)} copy(bf16[2,768,2,1024]{3,2,1,0:T(2,128)(2,1)} %param.24) | data formatting | bytes 12582912 | tf_op args[7]
  16.9 95.1 %forward.1 = (bf16[2560,768]{1,0:T(8,128)(2,1)}, bf16[2560,384]{1,0:T(8,128)(2,1)}, bf16[2560,384]{1,0:T(8,128)(2,1)}, bf16[768,1152]{1,0:T(8,128)(2,1)}, bf16[7...) custom-call(bf16[640,768]{1,0:T(8,128)(2,1)} %bitcast.31, ...), custom_call_target="tpu_custom_call" | custom-call | tf_op jit(solution)/shard_map/forward/pallas_call | solution.py:1260
  112.0 28.6 %experts.1 = (bf16[2560,768]{1,0:T(8,128)(2,1)}, bf16[2560,768]{1,0:T(8,128)(2,1)}) custom-call(s32[8,128]{1,0:T(8,128)} %get-tuple-element.44.starts, f32[8,2560]{1,0:T(8,128)} %get-tuple-element.45.place_row, f32[2560,128]{1,0:T(8,128)} %get-tuple-element.46.place_hbm, bf16[2560,128]{1,0:T(8,128)(2,1)} %get-tuple-element.47.weight_hbm, ...), custom_call_target="tpu_custom_call" | custom-call | tf_op jit(solution)/shard_map/experts/pallas_call | solution.py:267
  140.6 117.9 %backward.1 = (bf16[640,768]{1,0:T(8,128)(2,1)}, f32[640,768]{1,0:T(8,128)}, f32[2,240,128]{2,1,0:T(8,128)}) custom-call(bf16[2560,768]{1,0:T(8,128)(2,1)} %get-tuple-element.50.moe_out, bf16[2560,768]{1,0:T(8,128)(2,1)} %get-tuple-element.51.moe_back, bf16[2560,768]{1,0:T(8,128)(2,1)} %get-tuple-element.52.n1_hbm, ...), custom_call_target="tpu_custom_call" | custom-call | tf_op jit(solution)/shard_map/backward/pallas_call | solution.py:2182
  258.6 0.0 copy-start.2
  258.6 0.0 copy-start
  258.6 3.4 %add_bitcast_fusion = f32[1,640,768]{2,1,0:T(8,128)} fusion(f32[640,768]{1,0:T(8,128)} %get-tuple-element.43.resid_hbm, bf16[640,768]{1,0:T(8,128)(2,1)} %get-tuple-element.80), kind=kLoop, calls=%fused_computation.1 | loop fusion | flops 983040 | bytes 4915200 | tf_op jit(solution)/shard_map/broadcast_in_dim | solution.py:2390
  262.0 0.0 copy-done.2
  262.0 0.8 copy.30
  262.8 0.0 copy-done
  262.8 1.3 copy.33
  (2 shorter events, 0.0 us)
Async XLA Ops:
  0.6 7.7 %copy-start.1 = (bf16[192,2,1024]{2,1,0:T(2,128)(2,1)S(1)}, bf16[192,2,1024]{2,1,0:T(2,128)(2,1)}, u32[]{:S(2)}) copy-start(bf16[192,2,1024]{2,1,0:T(2,128)(2,1)} %param.22) | copy-start | bytes 2359300
  258.6 3.4 %copy-start.2 = (f32[2,240,128]{2,1,0:T(8,128)S(1)}, f32[2,240,128]{2,1,0:T(8,128)}, u32[]{:S(2)}) copy-start(f32[2,240,128]{2,1,0:T(8,128)} %get-tuple-element.82) | copy-start | bytes 737284
  258.6 4.2 %copy-start = (f32[640,768]{1,0:T(8,128)S(1)}, f32[640,768]{1,0:T(8,128)}, u32[]{:S(2)}) copy-start(f32[640,768]{1,0:T(8,128)} %get-tuple-element.81) | copy-start | bytes 5898244
